TPU v7x, 32 devices: a whole 2x2x4 slice. The times are simulated.
32 devices in a mesh: dom: 4 (over y, core), event: 8 (over z, x).
Axes of the slice: x: 2, y: 2, z: 4, core: 2. Of those that a mesh axis runs over, the one named last changes fastest.
Arguments:
- adjoint_state: float32 [8, 9, 64, 3072], P('event', None, None, 'dom'), may hold values from -6 to 6
- forward_velocity: float32 [8, 3, 3, 64, 3072], P('event', None, None, None, 'dom'), may hold values from -6 to 6
- density: float32 [64, 3072], P(None, 'dom'), may hold values from 1 to 3
- lame_lambda: float32 [64, 3072], P(None, 'dom'), may hold values from 0.5 to 2
- shear_modulus: float32 [64, 3072], P(None, 'dom'), may hold values from 0.5 to 2
- neighbour: int32 [6, 3072], P(None, 'dom'), may hold values from -1 to 1647, as said below
- send_list: int32 [2, 1760], P(None, 'dom'), may hold values from -1 to 4607, as said below
Outputs:
- adjoint_velocity: float32 [8, 3, 64, 3072], P('event', None, None, 'dom')
- kernels: float32 [3, 4, 49152], P(None, 'dom', 'event')
Inputs may be any that keep to these rules, and one draw needn't show every extreme that they name: `neighbour`: codes 0 to 767 name a slot of the same block, and then that slot's face f xor 1 names this face back; a code 768 + j names position j of row 1 of block b - 1 in send_list, a code 768 + 440 + j position j of row 0 of block b + 1, and such a position holds the partner face; -1 marks outer faces and every face of an unused slot. Every used slot has at least one face with a code other than -1; the used slots of a block come first. In every draw some block uses all 768 slots. `send_list`: positions b * 440 to (b + 1) * 440 - 1 belong to block b: row 0 lists the faces of b whose partner lies in block b - 1, row 1 those whose partner lies in block b + 1, each as f * 768 + s, used positions first and -1 after them. In every draw some block fills all 440 positions of row 0 and some block all 440 of row 1.
All inputs are finite; a program needn't handle non-finite values.
Results may differ from a plain program's by a relative error of at most 0.0001.
Values sent between devices are 32-bit elements; how exact they have to be, the bound alone decides.
No kernel may reach another device: no remote copies, remote signals or barrier semaphores. Data moves between devices by JAX's collectives and lax.ppermute only.
A program may use at most 128 MiB of HBM per device.

v0:
```python
import functools
import math

import jax
import jax.numpy as jnp
import numpy as np
from jax import lax
from jax.experimental import pallas as pl
from jax.experimental.pallas import tpu as pltpu
from jax.sharding import PartitionSpec as P

time_step = 0.02
lift_half = 3.0
symmetric_index = ((0, 3, 4), (3, 1, 5), (4, 5, 2))
f32 = jnp.float32
bf16 = jnp.bfloat16
CHUNK = 256
MAIN = 384
TAIL = 64
HALO = 512
VMEM_LIMIT = 40 * 2**20


def lobatto_diff():
    points = [-1.0, -1.0 / math.sqrt(5.0), 1.0 / math.sqrt(5.0), 1.0]
    weights = [
        1.0 / math.prod([points[t] - points[o] for o in range(4) if o != t]) for t in range(4)
    ]
    offdiag = [
        [
            0.0 if t == s else weights[s] / weights[t] / (points[t] - points[s])
            for s in range(4)
        ]
        for t in range(4)
    ]
    return np.array(
        [[-sum(offdiag[t]) if t == s else offdiag[t][s] for s in range(4)] for t in range(4)],
        dtype=np.float64,
    )


def kron3(first, second, third):
    return np.kron(np.kron(first, second), third)


def deriv_parts(inner):
    matrix = lobatto_diff()
    if inner:
        matrix = matrix + np.diag([lift_half, 0.0, 0.0, -lift_half])
    matrix = matrix.astype(np.float32)
    eye = np.eye(4, dtype=np.float32)
    stack = [kron3(matrix, eye, eye), kron3(eye, matrix, eye), kron3(eye, eye, matrix)]
    high = [np.asarray(m.astype(bf16)) for m in stack]
    low = [np.asarray((m - h.astype(np.float32)).astype(bf16)) for m, h in zip(stack, high)]
    return [h.astype(np.float32) for h in high], [l.astype(np.float32) for l in low]


def tables():
    high, low = deriv_parts(True)
    plain_high, plain_low = deriv_parts(False)

    def rows(upper, lower):
        return np.concatenate(
            [np.concatenate([upper[j], upper[j], lower[j]], axis=1) for j in range(3)], axis=0
        )

    vel = rows(high, low)
    fwd = rows(plain_high, plain_low)
    div = np.concatenate([m for j in range(3) for m in (high[j], high[j], low[j])], axis=1)
    return {
        name: np.asarray(value).astype(bf16) for name, value in dict(vel=vel, fwd=fwd, div=div).items()
    }


def split(value):
    high = value.astype(bf16)
    return high, (value - high.astype(f32)).astype(bf16)


def mm(left, right):
    return jnp.dot(left, right, preferred_element_type=f32)


def onehot(row, depth):
    ids = lax.broadcasted_iota(jnp.int32, (depth, row.shape[-1]), 0)
    return jnp.where(ids == row, 1.0, 0.0).astype(bf16)


def chunks(width):
    return [slice(c, c + CHUNK) for c in range(0, width, CHUNK)]


def top_half(shape):
    return lax.broadcasted_iota(jnp.int32, shape, 0) < 4


def tiles_of(lanes):
    return [(lanes.start // 128 + t, slice(128 * t, 128 * t + 128)) for t in range(CHUNK // 128)]


def z_faces(value, stage, lanes):
    low, high = [], []
    for tile, at in tiles_of(lanes):
        stage[tile] = value[:, at]
        low.append(stage[tile, pl.ds(0, 16, stride=4)])
        high.append(stage[tile, pl.ds(3, 16, stride=4)])
    return jnp.concatenate(low, axis=1), jnp.concatenate(high, axis=1)


def xy_faces(value):
    top = top_half((8, value.shape[1]))

    def rows(at):
        return value[at:at + 8]

    def turned(at):
        return pltpu.roll(value[at:at + 8], 4, 0)

    low_y = [jnp.where(top, rows(at), turned(at + 16)) for at in (0, 32)]
    high_y = [jnp.where(top, turned(at), rows(at + 16)) for at in (8, 40)]
    return [
        value[0:16],
        value[48:64],
        jnp.concatenate(low_y, axis=0),
        jnp.concatenate(high_y, axis=0),
    ]


def spread(faces, comp, scratch, lanes):
    low_x, high_x, low_y, high_y, low_z, high_z = (
        p[16 * comp:16 * comp + 16] for p in faces
    )
    width = low_x.shape[1]
    top = top_half((8, width))
    none = jnp.zeros((8, width), f32)
    along_y = []
    for a in range(4):
        first = low_y[8 * (a // 2):8 * (a // 2) + 8]
        second = high_y[8 * (a // 2):8 * (a // 2) + 8]
        first, second = (
            (pltpu.roll(first, 4, 0), second) if a % 2 else (first, pltpu.roll(second, 4, 0))
        )
        along_y += [jnp.where(top, first, none), jnp.where(top, none, second)]
    along_z = []
    for tile, at in tiles_of(lanes):
        scratch[comp, tile, pl.ds(0, 16, stride=4)] = low_z[:, at]
        scratch[comp, tile, pl.ds(3, 16, stride=4)] = high_z[:, at]
        along_z.append(scratch[comp, tile])
    return (
        jnp.concatenate([low_x, none, none, none, none, high_x], axis=0),
        jnp.concatenate(along_y, axis=0),
        jnp.concatenate(along_z, axis=1),
    )


def signed(fields):
    along_x, along_y, along_z = fields
    width = along_x.shape[1]
    node = lax.broadcasted_iota(jnp.int32, (8, width), 0) & 3
    sign = jnp.where(node == 0, -lift_half, lift_half)
    return (
        jnp.concatenate([-lift_half * along_x[0:16], along_x[16:48], lift_half * along_x[48:64]], axis=0),
        jnp.concatenate(
            [(lift_half if b % 2 else -lift_half) * along_y[8 * b:8 * b + 8] for b in range(8)], axis=0
        ),
        jnp.concatenate([sign * along_z[8 * b:8 * b + 8] for b in range(8)], axis=0),
    )


def holders(width):
    node = lax.broadcasted_iota(jnp.int32, (64, width), 0)
    total = jnp.zeros((64, width), f32)
    for index in (node >> 4, (node >> 2) & 3, node & 3):
        total = total + jnp.where((index == 0) | (index == 3), 1.0, 0.0)
    return total


def gather_tile(source, lane):
    lane = jnp.broadcast_to(lane, (8, 128))
    return jnp.concatenate(
        [jnp.take_along_axis(source[r:r + 8], lane, axis=1) for r in range(0, 48, 8)], axis=0
    )


def halo_faces(lhs, tail, keys, hots, lanes, width):
    blocks = 2 * MAIN // CHUNK
    first = width // CHUNK
    out = []
    for f in range(6):
        key = keys[f:f + 1]
        got = mm(lhs, hots[f, :, lanes])
        which = key >> 8
        late = jnp.concatenate(
            [gather_tile(tail, key[:, t:t + 128] & 127) for t in range(0, CHUNK, 128)], axis=1
        )
        total = jnp.where(which == first + blocks, late, 0.0)
        for a in range(blocks):
            both = got[48 * a:48 * a + 48] + got[48 * (blocks + a):48 * (blocks + a) + 48]
            total = jnp.where(which == first + a, both, total)
        out.append(total)
    return out


def halo_lhs(recv_one, recv_two):
    whole = jnp.concatenate([recv_one[:, 0:MAIN], recv_two[:, 0:MAIN]], axis=1)
    high, low = split(jnp.concatenate([whole[:, s] for s in chunks(2 * MAIN)], axis=0))
    tail = jnp.concatenate(
        [recv_one[:, MAIN:MAIN + TAIL], recv_two[:, MAIN:MAIN + TAIL]], axis=1
    )
    return jnp.concatenate([high, low], axis=0), tail


def local_faces(traces, keys, hots, lanes, own_sign):
    width = traces.shape[1]
    blocks = width // CHUNK
    out = []
    for f in range(6):
        key = keys[f:f + 1]
        other = 48 * (f ^ 1)
        lhs = jnp.concatenate(
            [traces[p + other:p + other + 48, s] for p in (0, 288) for s in chunks(width)], axis=0
        )
        got = mm(lhs, hots[f, :, lanes])
        which = key >> 8
        own = traces[48 * f:48 * f + 48, lanes].astype(f32)
        own = own + traces[288 + 48 * f:288 + 48 * f + 48, lanes].astype(f32)
        total = jnp.where(which < 0, own_sign * own, 0.0)
        for a in range(blocks):
            both = got[48 * a:48 * a + 48] + got[48 * (blocks + a):48 * (blocks + a) + 48]
            total = jnp.where(which == a, both, total)
        out.append(total)
    return out


def put_traces(traces, lanes, comp, face, value):
    at = 48 * face + 16 * comp
    traces[at:at + 16, lanes], traces[288 + at:288 + at + 16, lanes] = split(value)


def vel_traces(traces, lanes, velocity, stage):
    for i in range(3):
        faces = (*xy_faces(velocity[i]), *z_faces(velocity[i], stage.at[i], lanes))
        for f, value in enumerate(faces):
            put_traces(traces, lanes, i, f, value)


def str_traces(traces, lanes, stress, stage):
    faces = [xy_faces(stress[m]) for m in range(6)]
    for i in range(3):
        for f in range(4):
            put_traces(traces, lanes, i, f, faces[symmetric_index[i][f // 2]][f])
        for f, value in enumerate(z_faces(stress[symmetric_index[i][2]], stage.at[i], lanes)):
            put_traces(traces, lanes, i, 4 + f, value)


def pack(traces, values, picks, faces, late, send_one, send_two):
    width = traces.shape[1]
    pieces = []
    for s in chunks(2 * MAIN):
        face = faces[:, s]
        got = mm(traces[...], picks[:, s])
        total = jnp.zeros((48, CHUNK), f32)
        for f in range(6):
            both = got[48 * f:48 * f + 48] + got[288 + 48 * f:288 + 48 * f + 48]
            total = jnp.where(face == f, both, total)
        pieces.append(total)
    whole = jnp.concatenate(pieces, axis=1)
    send_one[:, 0:MAIN] = whole[:, 0:MAIN]
    send_two[:, 0:MAIN] = whole[:, MAIN:2 * MAIN]
    for at in range(0, 288, 16):
        values[at:at + 16] = (
            traces[at:at + 16].astype(f32) + traces[288 + at:288 + at + 16].astype(f32)
        )
    key = late[...]
    lane = key & 127
    which = jnp.broadcast_to(key >> 7, (48, 128))
    total = jnp.zeros((48, 128), f32)
    for f in range(6):
        for a in range(width // 128):
            got = gather_tile(values[48 * f:48 * f + 48, 128 * a:128 * a + 128], lane)
            total = jnp.where(which == f * (width // 128) + a, got, total)
    none = jnp.zeros((48, HALO - MAIN - TAIL), f32)
    send_one[:, MAIN:HALO] = jnp.concatenate([total[:, 0:TAIL], none], axis=1)
    send_two[:, MAIN:HALO] = jnp.concatenate([total[:, TAIL:2 * TAIL], none], axis=1)


def rate_of(grad, lame, shear):
    trace = lame * (grad[0][0] + grad[1][1] + grad[2][2])
    return [
        trace + 2.0 * shear * grad[0][0],
        trace + 2.0 * shear * grad[1][1],
        trace + 2.0 * shear * grad[2][2],
        shear * (grad[0][1] + grad[1][0]),
        shear * (grad[0][2] + grad[2][0]),
        shear * (grad[1][2] + grad[2][1]),
    ]


def lift_velocity(plus, scratch, lanes):
    grad, jump = [], []
    for i in range(3):
        fields = spread(plus, i, scratch, lanes)
        grad.append(signed(fields))
        jump.append(lift_half * (fields[0] + fields[1] + fields[2]))
    return grad, jump


def lift_stress(plus, scratch, lanes):
    out = []
    for i in range(3):
        along_x, along_y, along_z = signed(spread(plus, i, scratch, lanes))
        out.append(along_x + along_y + along_z)
    return out


def start_kernel(
    even, state_hbm, neighbour_hbm, send_list_hbm,
    velocity, stress, keys, picks, faces, late, traces, send_one, send_two,
    state, neighbour, send_list, values, stage, sems,
):
    copies = [
        pltpu.make_async_copy(source, target, sems.at[k])
        for k, (source, target) in enumerate((
            (neighbour_hbm, neighbour), (send_list_hbm, send_list),
            (state_hbm.at[0:3], state.at[0:3]), (state_hbm.at[3:9], state.at[3:9]),
        ))
    ]
    for copy in copies:
        copy.start()
    for copy in copies[0:2]:
        copy.wait()
    width = neighbour.shape[1]
    cap = send_list.shape[1]
    is_even = even[0] == 1
    code = neighbour[...]
    low = code < width + cap
    at = code - width - jnp.where(low, 0, cap)
    second = jnp.where(low == is_even, 0, 1)
    place = jnp.where(
        at < MAIN, at + MAIN * second, at - MAIN + 2 * MAIN + TAIL * second
    )
    keys[...] = jnp.where(code < width, code, width + place)
    valid = jnp.where(jnp.max(code, axis=0, keepdims=True) >= 0, 1.0, 0.0)
    entries = send_list[...]
    entries = jnp.concatenate(
        [entries, jnp.full((2, MAIN + TAIL - cap), -1, jnp.int32)], axis=1
    )
    one, two = entries[0:1], entries[1:2]
    one, two = jnp.where(is_even, one, two), jnp.where(is_even, two, one)
    late[...] = jnp.concatenate([one[:, MAIN:], two[:, MAIN:]], axis=1)
    main = jnp.concatenate([one[:, 0:MAIN], two[:, 0:MAIN]], axis=1)
    face = jnp.zeros_like(main)
    for f in range(1, 6):
        face = face + jnp.where(main >= f * width, 1, 0)
    faces[...] = face
    slots = main - face * width
    for s in chunks(2 * MAIN):
        picks[:, s] = onehot(slots[:, s], width)
    copies[2].wait()
    for lanes in chunks(width):
        mask = valid[:, lanes]
        now = [state[i, :, lanes] * mask for i in range(3)]
        for i in range(3):
            velocity[i, :, lanes] = now[i]
        vel_traces(traces, lanes, now, stage)
    pack(traces, values, picks, faces, late, send_one, send_two)
    copies[3].wait()
    for lanes in chunks(width):
        for i in range(6):
            stress[i, :, lanes] = state[3 + i, :, lanes] * valid[:, lanes]


def vel_local_kernel(
    step, velocity, stress, traces, keys, lame, shear, vel, *rest,
):
    total = None
    *rest, scratch = rest
    scratch[...] = jnp.zeros(scratch.shape, f32)
    if step < 0:
        stress_out, jump_out, hots = rest
    elif step == 0:
        hots, forward, stress_out, jump_out, total_out = rest
    else:
        hots, forward, total, stress_out, jump_out, total_out = rest
    width = velocity.shape[2]
    for lanes in chunks(width):
        if step < 0:
            for f in range(6):
                hots[f, :, lanes] = onehot(keys[f:f + 1, lanes] & (CHUNK - 1), CHUNK)
        plus = local_faces(traces, keys[:, lanes], hots, lanes, 1.0)
        grad, jump = lift_velocity(plus, scratch, lanes)
        own = -lift_half * holders(CHUNK)
        whole = []
        for i in range(3):
            now = velocity[i, :, lanes]
            high, low = split(now)
            got = mm(vel[...], jnp.concatenate([high, low, high], axis=0))
            whole.append([got[64 * j:64 * j + 64] + grad[i][j] for j in range(3)])
            jump_out[i, :, lanes] = own * now + jump[i]
        rate = rate_of(whole, lame[:, lanes], shear[:, lanes])
        for m in range(6):
            stress_out[m, :, lanes] = stress[m, :, lanes] + time_step * rate[m]
        if step >= 0:
            term = rho_term(forward, step, velocity, lanes)
            total_out[:, lanes] = term if total is None else total[:, lanes] + term


def rho_term(forward, step, velocity, lanes):
    acc = forward[step, 0, :, lanes] * velocity[0, :, lanes]
    acc = acc + forward[step, 1, :, lanes] * velocity[1, :, lanes]
    acc = acc + forward[step, 2, :, lanes] * velocity[2, :, lanes]
    return -time_step * acc


def vel_halo_kernel(
    stress, jump, recv_one, recv_two, keys, hots, picks, faces, late, lame, shear,
    stress_out, jump_out, traces, send_one, send_two, values, scratch, stage,
):
    width = stress.shape[2]
    scratch[...] = jnp.zeros(scratch.shape, f32)
    lhs, tail = halo_lhs(recv_one, recv_two)
    for lanes in chunks(width):
        plus = halo_faces(lhs, tail, keys[:, lanes], hots, lanes, width)
        grad, more = lift_velocity(plus, scratch, lanes)
        rate = rate_of(grad, lame[:, lanes], shear[:, lanes])
        now = [stress[m, :, lanes] + time_step * rate[m] for m in range(6)]
        for m in range(6):
            stress_out[m, :, lanes] = now[m]
        for i in range(3):
            jump_out[i, :, lanes] = jump[i, :, lanes] + more[i]
        str_traces(traces, lanes, now, stage)
    pack(traces, values, picks, faces, late, send_one, send_two)


def str_local_kernel(
    step, velocity, stress, jump, traces, keys, hots, density, lame, shear, forward, div, fwd, *rest,
):
    *rest, scratch = rest
    scratch[...] = jnp.zeros(scratch.shape, f32)
    if len(rest) == 2:
        total = None
        velocity_out, total_out = rest
    else:
        total, velocity_out, total_out = rest
    width = velocity.shape[2]
    for lanes in chunks(width):
        plus = local_faces(traces, keys[:, lanes], hots, lanes, -1.0)
        lifted = lift_stress(plus, scratch, lanes)
        now = [stress[m, :, lanes] for m in range(6)]
        pieces = [split(s) for s in now]
        rho = density[:, lanes]
        impedance = jnp.sqrt(rho * (lame[:, lanes] + 2.0 * shear[:, lanes]))
        scale = time_step / rho
        for i in range(3):
            rows = []
            for m in symmetric_index[i]:
                rows += [pieces[m][0], pieces[m][1], pieces[m][0]]
            got = mm(div[...], jnp.concatenate(rows, axis=0))
            velocity_out[i, :, lanes] = velocity[i, :, lanes] + scale * (
                got + lifted[i] + impedance * jump[i, :, lanes]
            )
        grad = []
        for i in range(3):
            high, low = split(forward[step, i, :, lanes])
            got = mm(fwd[...], jnp.concatenate([high, low, high], axis=0))
            grad.append([got[64 * j:64 * j + 64] for j in range(3)])
        diag = (grad[0][0], grad[1][1], grad[2][2])
        lame_term = -time_step * (diag[0] + diag[1] + diag[2]) * (now[0] + now[1] + now[2])
        shear_term = (-2.0 * time_step) * (
            diag[0] * now[0]
            + diag[1] * now[1]
            + diag[2] * now[2]
            + (grad[0][1] + grad[1][0]) * now[3]
            + (grad[0][2] + grad[2][0]) * now[4]
            + (grad[1][2] + grad[2][1]) * now[5]
        )
        for m, term in enumerate((lame_term, shear_term)):
            rows = total_out.shape[2]
            for e in range(total_out.shape[0]):
                share = term[rows * e:rows * e + rows]
                if total is not None:
                    share = total[e, m, :, lanes] + share
                total_out[e, m, :, lanes] = share


def str_halo_kernel(
    velocity, recv_one, recv_two, keys, hots, picks, faces, late, density,
    velocity_out, traces, send_one, send_two, values, scratch, stage,
):
    halo_velocity(velocity, recv_one, recv_two, keys, hots, density, velocity_out, traces, scratch, stage)
    pack(traces, values, picks, faces, late, send_one, send_two)


def last_kernel(
    step, velocity, recv_one, recv_two, keys, hots, density, forward, other, *rest
):
    *total, velocity_out, total_out, scratch = rest
    total = total[0] if total else None
    halo_velocity(velocity, recv_one, recv_two, keys, hots, density, velocity_out, None, scratch, None)
    for lanes in chunks(velocity.shape[2]):
        term = rho_term(forward, step, velocity_out, lanes)
        if total is not None:
            term = total[:, lanes] + term
        rows = total_out.shape[2]
        for e in range(total_out.shape[0]):
            total_out[e, 0, :, lanes] = term[rows * e:rows * e + rows]
            for m in range(2):
                total_out[e, m + 1, :, lanes] = other[e, m, :, lanes]


def event_sum_kernel(parts, out):
    width = parts.shape[3]
    for m in range(3):
        total = parts[0, m]
        for e in range(1, parts.shape[0]):
            total = total + parts[e, m]
        for k in range(total.shape[0]):
            out[m, :, k * width:(k + 1) * width] = total[k:k + 1]


def halo_velocity(
    velocity, recv_one, recv_two, keys, hots, density, velocity_out, traces, scratch, stage
):
    width = velocity.shape[2]
    scratch[...] = jnp.zeros(scratch.shape, f32)
    lhs, tail = halo_lhs(recv_one, recv_two)
    for lanes in chunks(width):
        plus = halo_faces(lhs, tail, keys[:, lanes], hots, lanes, width)
        lifted = lift_stress(plus, scratch, lanes)
        scale = time_step / density[:, lanes]
        now = [velocity[i, :, lanes] + scale * lifted[i] for i in range(3)]
        for i in range(3):
            velocity_out[i, :, lanes] = now[i]
        if traces is not None:
            vel_traces(traces, lanes, now, stage)


def call(name, kernel, args, outs, specs=None, cost=0, scratch=()):
    whole = pl.BlockSpec(memory_space=pltpu.VMEM)
    specs = specs or {}
    return pl.pallas_call(
        kernel,
        name=name,
        in_specs=[specs.get(k, whole) for k in range(len(args))],
        out_specs=[whole] * len(outs),
        out_shape=[jax.ShapeDtypeStruct(s, d) for s, d in outs],
        scratch_shapes=list(scratch),
        compiler_params=pltpu.CompilerParams(vmem_limit_bytes=VMEM_LIMIT),
        cost_estimate=pl.CostEstimate(flops=cost, bytes_accessed=6_000_000, transcendentals=0),
    )(*args)


def swap(sent, axis):
    count = lax.axis_size(axis)
    got = []
    for first, value in enumerate(sent):
        pairs = []
        for low in range(1 - first, count - 1, 2):
            pairs += [(low, low + 1), (low + 1, low)]
        got.append(lax.ppermute(value, axis, pairs))
    return got


def local(
    adjoint_state, forward_velocity, density, lame_lambda, shear_modulus, neighbour, send_list
):
    width = density.shape[1]
    steps = forward_velocity.shape[1]
    table = {k: jnp.asarray(v) for k, v in tables().items()}
    state = adjoint_state[0]
    forward = forward_velocity[0]
    even = (1 - lax.axis_index("dom") % 2).astype(jnp.int32).reshape(1)

    nodal = pltpu.VMEM((3, width // 128, 64, 128), f32)
    values = pltpu.VMEM((288, width), f32)
    field = ((64, width), f32)
    vector = ((3, 64, width), f32)
    tensor = ((6, 64, width), f32)
    count = lax.axis_size("event")
    shares = count if 64 % (8 * count) == 0 else 1
    two = ((shares, 2, 64 // shares, width), f32)
    three = ((shares, 3, 64 // shares, width), f32)
    trace = ((576, width), bf16)
    hot = ((6, CHUNK, width), bf16)
    sends = [((48, HALO), f32)] * 2
    lists = [((6, width), jnp.int32), ((width, 2 * MAIN), bf16),
             ((1, 2 * MAIN), jnp.int32), ((1, 2 * TAIL), jnp.int32)]

    velocity, stress, keys, picks, faces, late, traces, *sent = call(
        "start", start_kernel,
        (even, *(pltpu.with_memory_space_constraint(x, pltpu.HBM)
                for x in (state, neighbour, send_list))),
        [vector, tensor] + lists + [trace] + sends,
        specs={0: pl.BlockSpec(memory_space=pltpu.SMEM)}
        | {k: pl.BlockSpec(memory_space=pltpu.HBM) for k in range(1, 4)},
        scratch=[
            pltpu.VMEM(state.shape, f32), pltpu.VMEM(neighbour.shape, jnp.int32),
            pltpu.VMEM(send_list.shape, jnp.int32), values, nodal, pltpu.SemaphoreType.DMA((4,)),
        ],
    )
    rho_total = other_total = hots = None
    for n in range(steps):
        recv = swap(sent, "dom")
        args = [velocity, stress, traces, keys, lame_lambda, shear_modulus,
                table["vel"]]
        outs = [tensor, vector]
        if n:
            args += [hots, forward] + ([rho_total] if n > 1 else [])
            outs += [field]
        else:
            outs += [hot]
        stress, jump, more = call(
            "vel_local", functools.partial(vel_local_kernel, n - 1), args, outs, cost=4_000_000_000,
            scratch=[nodal],
        )
        if n:
            rho_total = more
        else:
            hots = more
        stress, jump, traces, *sent = call(
            "vel_halo", vel_halo_kernel,
            (stress, jump, *recv, keys, hots, picks, faces, late, lame_lambda, shear_modulus),
            [tensor, vector, trace] + sends, scratch=[values, nodal, nodal],
        )
        recv = swap(sent, "dom")
        args = [velocity, stress, jump, traces, keys, hots, density, lame_lambda, shear_modulus,
                forward, table["div"], table["fwd"]]
        if n:
            args += [other_total]
        velocity, other_total = call(
            "str_local", functools.partial(str_local_kernel, n), args, [vector, two],
            cost=4_000_000_000, scratch=[nodal],
        )
        if n < steps - 1:
            velocity, traces, *sent = call(
                "str_halo", str_halo_kernel,
                (velocity, *recv, keys, hots, picks, faces, late, density),
                [vector, trace] + sends, scratch=[values, nodal, nodal],
            )
        else:
            velocity, kernel_total = call(
                "last", functools.partial(last_kernel, n),
                (velocity, *recv, keys, hots, density, forward, other_total)
                + ((rho_total,) if n else ()),
                [vector, three], scratch=[nodal],
            )

    if shares == count:
        parts = lax.all_to_all(kernel_total, "event", 0, 0, tiled=True)
        kernels, = call(
            "event_sum", event_sum_kernel, (parts,), [((3, 1, 64 // count * width), f32)]
        )
    else:
        flat = kernel_total.reshape(3, -1)
        part = lax.psum_scatter(flat, "event", scatter_dimension=1, tiled=True)
        kernels = part.reshape(3, 1, -1)
    return velocity[None], kernels


def solution(mesh):
    placed = (
        P("event", None, None, "dom"),
        P("event", None, None, None, "dom"),
        P(None, "dom"),
        P(None, "dom"),
        P(None, "dom"),
        P(None, "dom"),
        P(None, "dom"),
    )
    return jax.shard_map(
        local,
        mesh=mesh,
        in_specs=placed,
        out_specs=(P("event", None, None, "dom"), P(None, "dom", "event")),
        check_vma=False,
    )
```

profile of v0, /device:TPU:0, one launch (start us, length us, event | category | flops | bytes accessed | tf_op | source)
XLA Modules:
  0.0 76.1 jit_solution(14849604999247986964)
XLA Ops:
  0.6 0.0 copy-start.5
  0.6 0.0 copy-start.1
  0.7 0.0 copy-start
  0.7 2.5 %start.1 = (f32[3,64,768]{2,1,0:T(8,128)S(1)}, f32[6,64,768]{2,1,0:T(8,128)S(1)}, s32[6,768]{1,0:T(8,128)S(1)}, bf16[768,768]{1,0:T(8,128)(2,1)S(1)}, s32[1,768]...) custom-call(s32[1]{0:T(128)} %bitcast.even, ...), custom_call_target="tpu_custom_call" | custom-call | bytes 6000000 | tf_op jit(solution)/shard_map/start/pallas_call | solution.py:541
  3.1 0.7 collective-permute-start
  3.8 4.4 %collective-permute-start.1 = (f32[48,512]{1,0:T(8,128)S(1)}, f32[48,512]{1,0:T(8,128)S(1)}, u32[]{:S(2)}, u32[]{:S(2)}) collective-permute-start(f32[48,512]{1,0:T(8,128)S(1)} %get-tuple-element.58), channel_id=1, source_target_pairs={{0,8},{8,0},{16,24},{24,16},{1,9},{9,1},{17,25},{25,17},{2,10},{10... | collective-permute-start | bytes 294920 | tf_op jit(solution)/shard_map/ppermute | solution.py:560
  8.2 0.0 copy-done.5
  8.2 0.0 copy-done.1
  8.2 0.0 copy-done
  8.2 1.8 %vel_local.3 = (f32[6,64,768]{2,1,0:T(8,128)S(1)}, f32[3,64,768]{2,1,0:T(8,128)S(1)}, bf16[6,256,768]{2,1,0:T(8,128)(2,1)S(1)}) custom-call(f32[3,64,768]{2,1,0:T(8,128)S(1)} %get-tuple-element.51.velocity, f32[6,64,768]{2,1,0:T(8,128)S(1)} %get-tuple-element.52.stress, bf16[576,768]{1,0:T(8,128)(2,1)S(1)} %get-tuple-element.53.traces, ...), custom_call_target="tpu_custom_call" | custom-call | flops 4000000000 | bytes 6000000 | tf_op jit(solution)/shard_map/vel_local/pallas_call | solution.py:541
  10.0 0.0 collective-permute-done.recv_one
  10.0 0.0 collective-permute-done.1.recv_two
  10.0 0.0 copy-start.2
  10.0 0.0 copy-start.3
  10.0 0.0 copy-start.4
  10.0 0.0 copy-start.6
  10.0 2.3 %vel_halo.3 = (f32[6,64,768]{2,1,0:T(8,128)S(1)}, f32[3,64,768]{2,1,0:T(8,128)S(1)}, bf16[576,768]{1,0:T(8,128)(2,1)S(1)}, f32[48,512]{1,0:T(8,128)S(1)}, f32[48,512]{1,0:T(8,128)S(1)}) custom-call(f32[6,64,768]{2,1,0:T(8,128)S(1)} %get-tuple-element.55.stress, f32[3,64,768]{2,1,0:T(8,128)S(1)} %get-tuple-element.56.jump, ...), custom_call_target="tpu_custom_call" | custom-call | bytes 6000000 | tf_op jit(solution)/shard_map/vel_halo/pallas_call | solution.py:541
  12.3 0.7 collective-permute-start.2
  13.0 3.4 %collective-permute-start.3 = (f32[48,512]{1,0:T(8,128)S(1)}, f32[48,512]{1,0:T(8,128)S(1)}, u32[]{:S(2)}, u32[]{:S(2)}) collective-permute-start(f32[48,512]{1,0:T(8,128)S(1)} %get-tuple-element.68), channel_id=1, source_target_pairs={{0,8},{8,0},{16,24},{24,16},{1,9},{9,1},{17,25},{25,17},{2,10},{10... | collective-permute-start | bytes 294920 | tf_op jit(solution)/shard_map/ppermute | solution.py:560
  16.4 0.0 copy-done.2
  16.4 0.0 copy-done.3
  16.4 0.0 copy-done.4
  16.4 0.0 copy-done.6
  16.4 1.9 %str_local.3 = (f32[3,64,768]{2,1,0:T(8,128)S(1)}, f32[8,2,8,768]{3,2,1,0:T(8,128)S(1)}) custom-call(f32[3,64,768]{2,1,0:T(8,128)S(1)} %get-tuple-element.51.velocity, f32[6,64,768]{2,1,0:T(8,128)S(1)} %get-tuple-element.63.stress, f32[3,64,768]{2,1,0:T(8,128)S(1)} %get-tuple-element.64.jump, bf16[576,768]{1,0:T(8,128)(2,1)S(1)} %get-tuple-element.65.traces, ...), custom_call_target="tpu_custom_call" | custom-call | flops 4000000000 | bytes 6000000 | tf_op jit(solution)/shard_map/str_local/pallas_call | solution.py:541
  18.3 0.0 collective-permute-done.2.recv_one
  18.3 0.0 collective-permute-done.3.recv_two
  18.3 2.1 %str_halo.2 = (f32[3,64,768]{2,1,0:T(8,128)S(1)}, bf16[576,768]{1,0:T(8,128)(2,1)S(1)}, f32[48,512]{1,0:T(8,128)S(1)}, f32[48,512]{1,0:T(8,128)S(1)}) custom-call(f32[3,64,768]{2,1,0:T(8,128)S(1)} %get-tuple-element.66.velocity, f32[48,512]{1,0:T(8,128)S(1)} %collective-permute-done.2.recv_one, f32[48,512]{1,0:T(8,128)S(1)} %collective-permute-done.3.recv_two, ...), custom_call_target="tpu_custom_call" | custom-call | bytes 6000000 | tf_op jit(solution)/shard_map/str_halo/pallas_call | solution.py:541
  20.4 0.7 collective-permute-start.4
  21.1 3.4 %collective-permute-start.5 = (f32[48,512]{1,0:T(8,128)S(1)}, f32[48,512]{1,0:T(8,128)S(1)}, u32[]{:S(2)}, u32[]{:S(2)}) collective-permute-start(f32[48,512]{1,0:T(8,128)S(1)} %get-tuple-element.74), channel_id=1, source_target_pairs={{0,8},{8,0},{16,24},{24,16},{1,9},{9,1},{17,25},{25,17},{2,10},{10... | collective-permute-start | bytes 294920 | tf_op jit(solution)/shard_map/ppermute | solution.py:560
  24.4 1.7 %vel_local.4 = (f32[6,64,768]{2,1,0:T(8,128)S(1)}, f32[3,64,768]{2,1,0:T(8,128)S(1)}, f32[64,768]{1,0:T(8,128)S(1)}) custom-call(f32[3,64,768]{2,1,0:T(8,128)S(1)} %get-tuple-element.69.velocity, f32[6,64,768]{2,1,0:T(8,128)S(1)} %get-tuple-element.63.stress, bf16[576,768]{1,0:T(8,128)(2,1)S(1)} %get-tuple-element.70.traces, ...), custom_call_target="tpu_custom_call" | custom-call | flops 4000000000 | bytes 6000000 | tf_op jit(solution)/shard_map/vel_local/pallas_call | solution.py:541
  26.1 0.0 collective-permute-done.4.recv_one
  26.1 0.0 collective-permute-done.5.recv_two
  26.2 2.3 %vel_halo.4 = (f32[6,64,768]{2,1,0:T(8,128)S(1)}, f32[3,64,768]{2,1,0:T(8,128)S(1)}, bf16[576,768]{1,0:T(8,128)(2,1)S(1)}, f32[48,512]{1,0:T(8,128)S(1)}, f32[48,512]{1,0:T(8,128)S(1)}) custom-call(f32[6,64,768]{2,1,0:T(8,128)S(1)} %get-tuple-element.71.stress, f32[3,64,768]{2,1,0:T(8,128)S(1)} %get-tuple-element.72.jump, ...), custom_call_target="tpu_custom_call" | custom-call | bytes 6000000 | tf_op jit(solution)/shard_map/vel_halo/pallas_call | solution.py:541
  28.5 0.8 %collective-permute-start.6 = (f32[48,512]{1,0:T(8,128)S(1)}, f32[48,512]{1,0:T(8,128)S(1)}, u32[]{:S(2)}, u32[]{:S(2)}) collective-permute-start(f32[48,512]{1,0:T(8,128)S(1)} %get-tuple-element.80), channel_id=1, source_target_pairs={{8,16},{16,8},{9,17},{17,9},{10,18},{18,10},{11,19},{19,11},{12,20... | collective-permute-start | bytes 294920 | tf_op jit(solution)/shard_map/ppermute | solution.py:560
  29.3 3.5 %collective-permute-start.7 = (f32[48,512]{1,0:T(8,128)S(1)}, f32[48,512]{1,0:T(8,128)S(1)}, u32[]{:S(2)}, u32[]{:S(2)}) collective-permute-start(f32[48,512]{1,0:T(8,128)S(1)} %get-tuple-element.81), channel_id=1, source_target_pairs={{0,8},{8,0},{16,24},{24,16},{1,9},{9,1},{17,25},{25,17},{2,10},{10... | collective-permute-start | bytes 294920 | tf_op jit(solution)/shard_map/ppermute | solution.py:560
  32.8 1.9 %str_local.4 = (f32[3,64,768]{2,1,0:T(8,128)S(1)}, f32[8,2,8,768]{3,2,1,0:T(8,128)S(1)}) custom-call(f32[3,64,768]{2,1,0:T(8,128)S(1)} %get-tuple-element.69.velocity, f32[6,64,768]{2,1,0:T(8,128)S(1)} %get-tuple-element.75.stress, f32[3,64,768]{2,1,0:T(8,128)S(1)} %get-tuple-element.76.jump, bf16[576,768]{1,0:T(8,128)(2,1)S(1)} %get-tuple-element.77.traces, ...), custom_call_target="tpu_custom_call" | custom-call | flops 4000000000 | bytes 6000000 | tf_op jit(solution)/shard_map/str_local/pallas_call | solution.py:541
  34.7 0.0 collective-permute-done.6.recv_one
  34.8 0.0 collective-permute-done.7.recv_two
  34.8 2.1 %str_halo.3 = (f32[3,64,768]{2,1,0:T(8,128)S(1)}, bf16[576,768]{1,0:T(8,128)(2,1)S(1)}, f32[48,512]{1,0:T(8,128)S(1)}, f32[48,512]{1,0:T(8,128)S(1)}) custom-call(f32[3,64,768]{2,1,0:T(8,128)S(1)} %get-tuple-element.79.velocity, f32[48,512]{1,0:T(8,128)S(1)} %collective-permute-done.6.recv_one, f32[48,512]{1,0:T(8,128)S(1)} %collective-permute-done.7.recv_two, ...), custom_call_target="tpu_custom_call" | custom-call | bytes 6000000 | tf_op jit(solution)/shard_map/str_halo/pallas_call | solution.py:541
  36.8 0.7 collective-permute-start.8
  37.5 3.2 %collective-permute-start.9 = (f32[48,512]{1,0:T(8,128)S(1)}, f32[48,512]{1,0:T(8,128)S(1)}, u32[]{:S(2)}, u32[]{:S(2)}) collective-permute-start(f32[48,512]{1,0:T(8,128)S(1)} %get-tuple-element.88), channel_id=1, source_target_pairs={{0,8},{8,0},{16,24},{24,16},{1,9},{9,1},{17,25},{25,17},{2,10},{10... | collective-permute-start | bytes 294920 | tf_op jit(solution)/shard_map/ppermute | solution.py:560
  40.7 1.7 %vel_local.5 = (f32[6,64,768]{2,1,0:T(8,128)S(1)}, f32[3,64,768]{2,1,0:T(8,128)S(1)}, f32[64,768]{1,0:T(8,128)S(1)}) custom-call(f32[3,64,768]{2,1,0:T(8,128)S(1)} %get-tuple-element.82.velocity, f32[6,64,768]{2,1,0:T(8,128)S(1)} %get-tuple-element.75.stress, bf16[576,768]{1,0:T(8,128)(2,1)S(1)} %get-tuple-element.83.traces, ...), custom_call_target="tpu_custom_call" | custom-call | flops 4000000000 | bytes 6000000 | tf_op jit(solution)/shard_map/vel_local/pallas_call | solution.py:541
  42.3 0.0 collective-permute-done.8.recv_one
  42.4 0.0 collective-permute-done.9.recv_two
  42.4 2.3 %vel_halo.5 = (f32[6,64,768]{2,1,0:T(8,128)S(1)}, f32[3,64,768]{2,1,0:T(8,128)S(1)}, bf16[576,768]{1,0:T(8,128)(2,1)S(1)}, f32[48,512]{1,0:T(8,128)S(1)}, f32[48,512]{1,0:T(8,128)S(1)}) custom-call(f32[6,64,768]{2,1,0:T(8,128)S(1)} %get-tuple-element.85.stress, f32[3,64,768]{2,1,0:T(8,128)S(1)} %get-tuple-element.86.jump, ...), custom_call_target="tpu_custom_call" | custom-call | bytes 6000000 | tf_op jit(solution)/shard_map/vel_halo/pallas_call | solution.py:541
  44.7 0.7 collective-permute-start.10
  45.3 3.6 %collective-permute-start.11 = (f32[48,512]{1,0:T(8,128)S(1)}, f32[48,512]{1,0:T(8,128)S(1)}, u32[]{:S(2)}, u32[]{:S(2)}) collective-permute-start(f32[48,512]{1,0:T(8,128)S(1)} %get-tuple-element.95), channel_id=1, source_target_pairs={{0,8},{8,0},{16,24},{24,16},{1,9},{9,1},{17,25},{25,17},{2,10},{10... | collective-permute-start | bytes 294920 | tf_op jit(solution)/shard_map/ppermute | solution.py:560
  48.9 1.9 %str_local.5 = (f32[3,64,768]{2,1,0:T(8,128)S(1)}, f32[8,2,8,768]{3,2,1,0:T(8,128)S(1)}) custom-call(f32[3,64,768]{2,1,0:T(8,128)S(1)} %get-tuple-element.82.velocity, f32[6,64,768]{2,1,0:T(8,128)S(1)} %get-tuple-element.89.stress, f32[3,64,768]{2,1,0:T(8,128)S(1)} %get-tuple-element.90.jump, bf16[576,768]{1,0:T(8,128)(2,1)S(1)} %get-tuple-element.91.traces, ...), custom_call_target="tpu_custom_call" | custom-call | flops 4000000000 | bytes 6000000 | tf_op jit(solution)/shard_map/str_local/pallas_call | solution.py:541
  50.8 0.0 collective-permute-done.10.recv_one
  50.8 0.0 collective-permute-done.11.recv_two
  50.8 2.0 %last.1 = (f32[3,64,768]{2,1,0:T(8,128)}, f32[8,3,8,768]{3,2,1,0:T(8,128)S(1)}) custom-call(f32[3,64,768]{2,1,0:T(8,128)S(1)} %get-tuple-element.93.velocity, f32[48,512]{1,0:T(8,128)S(1)} %collective-permute-done.10.recv_one, f32[48,512]{1,0:T(8,128)S(1)} %collective-permute-done.11.recv_two, s32[6,768]{1,0:T(8,128)S(1)} %get-tuple-element.54.keys, ...), custom_call_target="tpu_custom_call" | custom-call | bytes 6000000 | tf_op jit(solution)/shard_map/last/pallas_call | solution.py:541
  52.8 22.6 %all_to_all.5.parts = f32[8,3,8,768]{3,2,1,0:T(8,128)S(1)} all-to-all(f32[8,3,8,768]{3,2,1,0:T(8,128)S(1)} %get-tuple-element.99), channel_id=1, replica_groups=mesh['dom'=4,'event'=8] {'event'}, dimensions={0} | all-to-all | bytes 1179648 | tf_op jit(solution)/shard_map/all_to_all | solution.py:649
  75.4 0.7 event_sum.1
Async XLA Ops:
  0.6 7.6 %copy-start.5 = (bf16[192,192]{1,0:T(8,128)(2,1)S(1)}, bf16[192,192]{1,0:T(8,128)(2,1)}, u32[]{:S(2)}) copy-start(bf16[192,192]{1,0:T(8,128)(2,1)} %constant.25.clone.vel) | copy-start | bytes 221188
  0.6 7.6 %copy-start.1 = (f32[64,768]{1,0:T(8,128)S(1)}, f32[64,768]{1,0:T(8,128)}, u32[]{:S(2)}) copy-start(f32[64,768]{1,0:T(8,128)} %shear.17) | copy-start | bytes 589828
  0.7 7.6 %copy-start = (f32[64,768]{1,0:T(8,128)S(1)}, f32[64,768]{1,0:T(8,128)}, u32[]{:S(2)}) copy-start(f32[64,768]{1,0:T(8,128)} %lame.17) | copy-start | bytes 589828
  3.1 6.8 %collective-permute-start = (f32[48,512]{1,0:T(8,128)S(1)}, f32[48,512]{1,0:T(8,128)S(1)}, u32[]{:S(2)}, u32[]{:S(2)}) collective-permute-start(f32[48,512]{1,0:T(8,128)S(1)} %get-tuple-element.57), channel_id=1, source_target_pairs={{8,16},{16,8},{9,17},{17,9},{10,18},{18,10},{11,19},{19,11},{12,20... | collective-permute-start | bytes 294920 | tf_op jit(solution)/shard_map/ppermute | solution.py:560
  3.8 6.2 %collective-permute-start.1 = (f32[48,512]{1,0:T(8,128)S(1)}, f32[48,512]{1,0:T(8,128)S(1)}, u32[]{:S(2)}, u32[]{:S(2)}) collective-permute-start(f32[48,512]{1,0:T(8,128)S(1)} %get-tuple-element.58), channel_id=1, source_target_pairs={{0,8},{8,0},{16,24},{24,16},{1,9},{9,1},{17,25},{25,17},{2,10},{10... | collective-permute-start | bytes 294920 | tf_op jit(solution)/shard_map/ppermute | solution.py:560
  10.0 6.4 %copy-start.2 = (f32[64,768]{1,0:T(8,128)S(1)}, f32[64,768]{1,0:T(8,128)}, u32[]{:S(2)}) copy-start(f32[64,768]{1,0:T(8,128)} %density.11) | copy-start | bytes 589828
  10.0 6.4 %copy-start.3 = (f32[1,3,3,64,768]{4,3,2,1,0:T(8,128)S(1)}, f32[1,3,3,64,768]{4,3,2,1,0:T(8,128)}, u32[]{:S(2)}) copy-start(f32[1,3,3,64,768]{4,3,2,1,0:T(8,128)} %param.11) | copy-start | bytes 5308420
  10.0 6.4 %copy-start.4 = (bf16[192,192]{1,0:T(8,128)(2,1)S(1)}, bf16[192,192]{1,0:T(8,128)(2,1)}, u32[]{:S(2)}) copy-start(bf16[192,192]{1,0:T(8,128)(2,1)} %constant.26.clone.fwd) | copy-start | bytes 221188
  10.0 6.4 %copy-start.6 = (bf16[64,576]{1,0:T(8,128)(2,1)S(1)}, bf16[64,576]{1,0:T(8,128)(2,1)}, u32[]{:S(2)}) copy-start(bf16[64,576]{1,0:T(8,128)(2,1)} %constant.27.clone.div) | copy-start | bytes 221188
  12.3 6.0 %collective-permute-start.2 = (f32[48,512]{1,0:T(8,128)S(1)}, f32[48,512]{1,0:T(8,128)S(1)}, u32[]{:S(2)}, u32[]{:S(2)}) collective-permute-start(f32[48,512]{1,0:T(8,128)S(1)} %get-tuple-element.67), channel_id=1, source_target_pairs={{8,16},{16,8},{9,17},{17,9},{10,18},{18,10},{11,19},{19,11},{12,20... | collective-permute-start | bytes 294920 | tf_op jit(solution)/shard_map/ppermute | solution.py:560
  13.0 5.3 %collective-permute-start.3 = (f32[48,512]{1,0:T(8,128)S(1)}, f32[48,512]{1,0:T(8,128)S(1)}, u32[]{:S(2)}, u32[]{:S(2)}) collective-permute-start(f32[48,512]{1,0:T(8,128)S(1)} %get-tuple-element.68), channel_id=1, source_target_pairs={{0,8},{8,0},{16,24},{24,16},{1,9},{9,1},{17,25},{25,17},{2,10},{10... | collective-permute-start | bytes 294920 | tf_op jit(solution)/shard_map/ppermute | solution.py:560
  20.4 5.7 %collective-permute-start.4 = (f32[48,512]{1,0:T(8,128)S(1)}, f32[48,512]{1,0:T(8,128)S(1)}, u32[]{:S(2)}, u32[]{:S(2)}) collective-permute-start(f32[48,512]{1,0:T(8,128)S(1)} %get-tuple-element.73), channel_id=1, source_target_pairs={{8,16},{16,8},{9,17},{17,9},{10,18},{18,10},{11,19},{19,11},{12,20... | collective-permute-start | bytes 294920 | tf_op jit(solution)/shard_map/ppermute | solution.py:560
  21.1 5.1 %collective-permute-start.5 = (f32[48,512]{1,0:T(8,128)S(1)}, f32[48,512]{1,0:T(8,128)S(1)}, u32[]{:S(2)}, u32[]{:S(2)}) collective-permute-start(f32[48,512]{1,0:T(8,128)S(1)} %get-tuple-element.74), channel_id=1, source_target_pairs={{0,8},{8,0},{16,24},{24,16},{1,9},{9,1},{17,25},{25,17},{2,10},{10... | collective-permute-start | bytes 294920 | tf_op jit(solution)/shard_map/ppermute | solution.py:560
  28.5 6.3 %collective-permute-start.6 = (f32[48,512]{1,0:T(8,128)S(1)}, f32[48,512]{1,0:T(8,128)S(1)}, u32[]{:S(2)}, u32[]{:S(2)}) collective-permute-start(f32[48,512]{1,0:T(8,128)S(1)} %get-tuple-element.80), channel_id=1, source_target_pairs={{8,16},{16,8},{9,17},{17,9},{10,18},{18,10},{11,19},{19,11},{12,20... | collective-permute-start | bytes 294920 | tf_op jit(solution)/shard_map/ppermute | solution.py:560
  29.3 5.5 %collective-permute-start.7 = (f32[48,512]{1,0:T(8,128)S(1)}, f32[48,512]{1,0:T(8,128)S(1)}, u32[]{:S(2)}, u32[]{:S(2)}) collective-permute-start(f32[48,512]{1,0:T(8,128)S(1)} %get-tuple-element.81), channel_id=1, source_target_pairs={{0,8},{8,0},{16,24},{24,16},{1,9},{9,1},{17,25},{25,17},{2,10},{10... | collective-permute-start | bytes 294920 | tf_op jit(solution)/shard_map/ppermute | solution.py:560
  36.8 5.5 %collective-permute-start.8 = (f32[48,512]{1,0:T(8,128)S(1)}, f32[48,512]{1,0:T(8,128)S(1)}, u32[]{:S(2)}, u32[]{:S(2)}) collective-permute-start(f32[48,512]{1,0:T(8,128)S(1)} %get-tuple-element.87), channel_id=1, source_target_pairs={{8,16},{16,8},{9,17},{17,9},{10,18},{18,10},{11,19},{19,11},{12,20... | collective-permute-start | bytes 294920 | tf_op jit(solution)/shard_map/ppermute | solution.py:560
  37.5 4.9 %collective-permute-start.9 = (f32[48,512]{1,0:T(8,128)S(1)}, f32[48,512]{1,0:T(8,128)S(1)}, u32[]{:S(2)}, u32[]{:S(2)}) collective-permute-start(f32[48,512]{1,0:T(8,128)S(1)} %get-tuple-element.88), channel_id=1, source_target_pairs={{0,8},{8,0},{16,24},{24,16},{1,9},{9,1},{17,25},{25,17},{2,10},{10... | collective-permute-start | bytes 294920 | tf_op jit(solution)/shard_map/ppermute | solution.py:560
  44.7 6.2 %collective-permute-start.10 = (f32[48,512]{1,0:T(8,128)S(1)}, f32[48,512]{1,0:T(8,128)S(1)}, u32[]{:S(2)}, u32[]{:S(2)}) collective-permute-start(f32[48,512]{1,0:T(8,128)S(1)} %get-tuple-element.94), channel_id=1, source_target_pairs={{8,16},{16,8},{9,17},{17,9},{10,18},{18,10},{11,19},{19,11},{12,20... | collective-permute-start | bytes 294920 | tf_op jit(solution)/shard_map/ppermute | solution.py:560
  45.3 5.5 %collective-permute-start.11 = (f32[48,512]{1,0:T(8,128)S(1)}, f32[48,512]{1,0:T(8,128)S(1)}, u32[]{:S(2)}, u32[]{:S(2)}) collective-permute-start(f32[48,512]{1,0:T(8,128)S(1)} %get-tuple-element.95), channel_id=1, source_target_pairs={{0,8},{8,0},{16,24},{24,16},{1,9},{9,1},{17,25},{25,17},{2,10},{10... | collective-permute-start | bytes 294920 | tf_op jit(solution)/shard_map/ppermute | solution.py:560
where the time goes:
time: 76.3 us; the launch traced here: 76.1 us
  Pallas kernels  26.8 us (35%)
  starting transfers between devices  25.6 us (34%)
  blocking collectives  22.6 us (30%)
  between operations  0.94 us (1%)
    pallas_call x14, Pallas kernels, call(): pl.pallas_call(kernel, name=name, in_specs=[specs.get(k, whole) for k in...  26.8 us
    ppermute x12, starting transfers between devices, swap(): got.append(lax.ppermute(value, axis, pairs))  25.6 us
    all_to_all x1, blocking collectives, local(): parts = lax.all_to_all(kernel_total, 'event', 0, 0, tiled=True)  22.6 us
  transfers between devices with their start and end apart: 12, of which 0 were waited for; matrix products, arithmetic and copies ran while one was open for 0% of the time, Pallas kernels for 14%

commit v1 on v0

--- a/solution.py
+++ b/solution.py
@@ -17,7 +17,8 @@
 CHUNK = 256
 MAIN = 384
 TAIL = 64
-HALO = 512
+SEND_MAIN = 48 * MAIN // 128
+SEND_ROWS = SEND_MAIN + 48 * TAIL // 128
 VMEM_LIMIT = 40 * 2**20
 
 
@@ -157,11 +158,12 @@
     along_x, along_y, along_z = fields
     width = along_x.shape[1]
     node = lax.broadcasted_iota(jnp.int32, (8, width), 0) & 3
-    sign = jnp.where(node == 0, -lift_half, lift_half)
+    sign = jnp.where(node == 0, -1.0, 1.0)
     return (
-        jnp.concatenate([-lift_half * along_x[0:16], along_x[16:48], lift_half * along_x[48:64]], axis=0),
+        jnp.concatenate([-along_x[0:16], along_x[16:64]], axis=0),
         jnp.concatenate(
-            [(lift_half if b % 2 else -lift_half) * along_y[8 * b:8 * b + 8] for b in range(8)], axis=0
+            [along_y[8 * b:8 * b + 8] if b % 2 else -along_y[8 * b:8 * b + 8] for b in range(8)],
+            axis=0,
         ),
         jnp.concatenate([sign * along_z[8 * b:8 * b + 8] for b in range(8)], axis=0),
     )
@@ -202,10 +204,18 @@
 
 
 def halo_lhs(recv_one, recv_two):
-    whole = jnp.concatenate([recv_one[:, 0:MAIN], recv_two[:, 0:MAIN]], axis=1)
-    high, low = split(jnp.concatenate([whole[:, s] for s in chunks(2 * MAIN)], axis=0))
+    tiles = [
+        recv[48 * t:48 * t + 48] for recv in (recv_one, recv_two) for t in range(MAIN // 128)
+    ]
+    blocks = [jnp.concatenate(tiles[t:t + 2], axis=1) for t in range(0, len(tiles), 2)]
+    high, low = split(jnp.concatenate(blocks, axis=0))
+    one, two = recv_one[SEND_MAIN:SEND_ROWS], recv_two[SEND_MAIN:SEND_ROWS]
     tail = jnp.concatenate(
-        [recv_one[:, MAIN:MAIN + TAIL], recv_two[:, MAIN:MAIN + TAIL]], axis=1
+        [
+            jnp.concatenate([one[:, 0:TAIL], two[:, 0:TAIL]], axis=1),
+            jnp.concatenate([one[:, TAIL:2 * TAIL], two[:, TAIL:2 * TAIL]], axis=1),
+        ],
+        axis=0,
     )
     return jnp.concatenate([high, low], axis=0), tail
 
@@ -232,25 +242,26 @@
     return out
 
 
-def put_traces(traces, lanes, comp, face, value):
+def put_traces(traces, values, lanes, comp, face, value):
     at = 48 * face + 16 * comp
+    values[at:at + 16, lanes] = value
     traces[at:at + 16, lanes], traces[288 + at:288 + at + 16, lanes] = split(value)
 
 
-def vel_traces(traces, lanes, velocity, stage):
+def vel_traces(traces, values, lanes, velocity, stage):
     for i in range(3):
         faces = (*xy_faces(velocity[i]), *z_faces(velocity[i], stage.at[i], lanes))
         for f, value in enumerate(faces):
-            put_traces(traces, lanes, i, f, value)
-
-
-def str_traces(traces, lanes, stress, stage):
+            put_traces(traces, values, lanes, i, f, value)
+
+
+def str_traces(traces, values, lanes, stress, stage):
     faces = [xy_faces(stress[m]) for m in range(6)]
     for i in range(3):
         for f in range(4):
-            put_traces(traces, lanes, i, f, faces[symmetric_index[i][f // 2]][f])
+            put_traces(traces, values, lanes, i, f, faces[symmetric_index[i][f // 2]][f])
         for f, value in enumerate(z_faces(stress[symmetric_index[i][2]], stage.at[i], lanes)):
-            put_traces(traces, lanes, i, 4 + f, value)
+            put_traces(traces, values, lanes, i, 4 + f, value)
 
 
 def pack(traces, values, picks, faces, late, send_one, send_two):
@@ -265,12 +276,9 @@
             total = jnp.where(face == f, both, total)
         pieces.append(total)
     whole = jnp.concatenate(pieces, axis=1)
-    send_one[:, 0:MAIN] = whole[:, 0:MAIN]
-    send_two[:, 0:MAIN] = whole[:, MAIN:2 * MAIN]
-    for at in range(0, 288, 16):
-        values[at:at + 16] = (
-            traces[at:at + 16].astype(f32) + traces[288 + at:288 + at + 16].astype(f32)
-        )
+    for t in range(MAIN // 128):
+        for first, send in ((0, send_one), (MAIN, send_two)):
+            send[48 * t:48 * t + 48] = whole[:, first + 128 * t:first + 128 * t + 128]
     key = late[...]
     lane = key & 127
     which = jnp.broadcast_to(key >> 7, (48, 128))
@@ -279,9 +287,9 @@
         for a in range(width // 128):
             got = gather_tile(values[48 * f:48 * f + 48, 128 * a:128 * a + 128], lane)
             total = jnp.where(which == f * (width // 128) + a, got, total)
-    none = jnp.zeros((48, HALO - MAIN - TAIL), f32)
-    send_one[:, MAIN:HALO] = jnp.concatenate([total[:, 0:TAIL], none], axis=1)
-    send_two[:, MAIN:HALO] = jnp.concatenate([total[:, TAIL:2 * TAIL], none], axis=1)
+    one, two = total[:, 0:TAIL], total[:, TAIL:2 * TAIL]
+    send_one[SEND_MAIN:SEND_ROWS] = jnp.concatenate([one[0:24], one[24:48]], axis=1)
+    send_two[SEND_MAIN:SEND_ROWS] = jnp.concatenate([two[0:24], two[24:48]], axis=1)
 
 
 def rate_of(grad, lame, shear):
@@ -301,7 +309,7 @@
     for i in range(3):
         fields = spread(plus, i, scratch, lanes)
         grad.append(signed(fields))
-        jump.append(lift_half * (fields[0] + fields[1] + fields[2]))
+        jump.append(fields[0] + fields[1] + fields[2])
     return grad, jump
 
 
@@ -362,7 +370,7 @@
         now = [state[i, :, lanes] * mask for i in range(3)]
         for i in range(3):
             velocity[i, :, lanes] = now[i]
-        vel_traces(traces, lanes, now, stage)
+        vel_traces(traces, values, lanes, now, stage)
     pack(traces, values, picks, faces, late, send_one, send_two)
     copies[3].wait()
     for lanes in chunks(width):
@@ -377,7 +385,7 @@
     *rest, scratch = rest
     scratch[...] = jnp.zeros(scratch.shape, f32)
     if step < 0:
-        stress_out, jump_out, hots = rest
+        stress_out, jump_out, hots, lame_scaled, shear_scaled = rest
     elif step == 0:
         hots, forward, stress_out, jump_out, total_out = rest
     else:
@@ -387,16 +395,18 @@
         if step < 0:
             for f in range(6):
                 hots[f, :, lanes] = onehot(keys[f:f + 1, lanes] & (CHUNK - 1), CHUNK)
+            lame_scaled[:, lanes] = (lift_half * time_step) * lame[:, lanes]
+            shear_scaled[:, lanes] = (lift_half * time_step) * shear[:, lanes]
         plus = local_faces(traces, keys[:, lanes], hots, lanes, 1.0)
         grad, jump = lift_velocity(plus, scratch, lanes)
-        own = -lift_half * holders(CHUNK)
+        count = holders(CHUNK)
         whole = []
         for i in range(3):
             now = velocity[i, :, lanes]
             high, low = split(now)
             got = mm(vel[...], jnp.concatenate([high, low, high], axis=0))
-            whole.append([got[64 * j:64 * j + 64] + grad[i][j] for j in range(3)])
-            jump_out[i, :, lanes] = own * now + jump[i]
+            whole.append([got[64 * j:64 * j + 64] + lift_half * grad[i][j] for j in range(3)])
+            jump_out[i, :, lanes] = jump[i] - count * now
         rate = rate_of(whole, lame[:, lanes], shear[:, lanes])
         for m in range(6):
             stress_out[m, :, lanes] = stress[m, :, lanes] + time_step * rate[m]
@@ -413,7 +423,7 @@
 
 
 def vel_halo_kernel(
-    stress, jump, recv_one, recv_two, keys, hots, picks, faces, late, lame, shear,
+    stress, jump, recv_one, recv_two, keys, hots, picks, faces, late, lame_scaled, shear_scaled,
     stress_out, jump_out, traces, send_one, send_two, values, scratch, stage,
 ):
     width = stress.shape[2]
@@ -422,13 +432,13 @@
     for lanes in chunks(width):
         plus = halo_faces(lhs, tail, keys[:, lanes], hots, lanes, width)
         grad, more = lift_velocity(plus, scratch, lanes)
-        rate = rate_of(grad, lame[:, lanes], shear[:, lanes])
-        now = [stress[m, :, lanes] + time_step * rate[m] for m in range(6)]
+        rate = rate_of(grad, lame_scaled[:, lanes], shear_scaled[:, lanes])
+        now = [stress[m, :, lanes] + rate[m] for m in range(6)]
         for m in range(6):
             stress_out[m, :, lanes] = now[m]
         for i in range(3):
             jump_out[i, :, lanes] = jump[i, :, lanes] + more[i]
-        str_traces(traces, lanes, now, stage)
+        str_traces(traces, values, lanes, now, stage)
     pack(traces, values, picks, faces, late, send_one, send_two)
 
 
@@ -437,9 +447,9 @@
 ):
     *rest, scratch = rest
     scratch[...] = jnp.zeros(scratch.shape, f32)
-    if len(rest) == 2:
+    if step == 0:
         total = None
-        velocity_out, total_out = rest
+        velocity_out, total_out, scale_out = rest
     else:
         total, velocity_out, total_out = rest
     width = velocity.shape[2]
@@ -451,13 +461,15 @@
         rho = density[:, lanes]
         impedance = jnp.sqrt(rho * (lame[:, lanes] + 2.0 * shear[:, lanes]))
         scale = time_step / rho
+        if step == 0:
+            scale_out[:, lanes] = lift_half * scale
         for i in range(3):
             rows = []
             for m in symmetric_index[i]:
                 rows += [pieces[m][0], pieces[m][1], pieces[m][0]]
             got = mm(div[...], jnp.concatenate(rows, axis=0))
             velocity_out[i, :, lanes] = velocity[i, :, lanes] + scale * (
-                got + lifted[i] + impedance * jump[i, :, lanes]
+                got + lift_half * (lifted[i] + impedance * jump[i, :, lanes])
             )
         grad = []
         for i in range(3):
@@ -484,28 +496,42 @@
 
 
 def str_halo_kernel(
-    velocity, recv_one, recv_two, keys, hots, picks, faces, late, density,
+    velocity, recv_one, recv_two, keys, hots, picks, faces, late, scale,
     velocity_out, traces, send_one, send_two, values, scratch, stage,
 ):
-    halo_velocity(velocity, recv_one, recv_two, keys, hots, density, velocity_out, traces, scratch, stage)
+    halo_velocity(
+        velocity, recv_one, recv_two, keys, hots, scale, velocity_out, traces, values, scratch, stage
+    )
     pack(traces, values, picks, faces, late, send_one, send_two)
 
 
 def last_kernel(
-    step, velocity, recv_one, recv_two, keys, hots, density, forward, other, *rest
+    step, velocity, recv_one, recv_two, keys, hots, scale, forward, other, *rest
 ):
-    *total, velocity_out, total_out, scratch = rest
+    *total, velocity_out, total_out, scratch, buffer, sems = rest
     total = total[0] if total else None
-    halo_velocity(velocity, recv_one, recv_two, keys, hots, density, velocity_out, None, scratch, None)
-    for lanes in chunks(velocity.shape[2]):
-        term = rho_term(forward, step, velocity_out, lanes)
+    rows = total_out.shape[2]
+    copies = []
+
+    def finish(lanes):
+        copy = pltpu.make_async_copy(
+            buffer.at[:, :, lanes], velocity_out.at[:, :, lanes], sems.at[len(copies)]
+        )
+        copy.start()
+        copies.append(copy)
+        term = rho_term(forward, step, buffer, lanes)
         if total is not None:
             term = total[:, lanes] + term
-        rows = total_out.shape[2]
         for e in range(total_out.shape[0]):
             total_out[e, 0, :, lanes] = term[rows * e:rows * e + rows]
             for m in range(2):
                 total_out[e, m + 1, :, lanes] = other[e, m, :, lanes]
+
+    halo_velocity(
+        velocity, recv_one, recv_two, keys, hots, scale, buffer, None, None, scratch, None, finish
+    )
+    for copy in copies:
+        copy.wait()
 
 
 def event_sum_kernel(parts, out):
@@ -519,7 +545,8 @@
 
 
 def halo_velocity(
-    velocity, recv_one, recv_two, keys, hots, density, velocity_out, traces, scratch, stage
+    velocity, recv_one, recv_two, keys, hots, scale, velocity_out, traces, values, scratch, stage,
+    finish=None,
 ):
     width = velocity.shape[2]
     scratch[...] = jnp.zeros(scratch.shape, f32)
@@ -527,22 +554,23 @@
     for lanes in chunks(width):
         plus = halo_faces(lhs, tail, keys[:, lanes], hots, lanes, width)
         lifted = lift_stress(plus, scratch, lanes)
-        scale = time_step / density[:, lanes]
-        now = [velocity[i, :, lanes] + scale * lifted[i] for i in range(3)]
+        now = [velocity[i, :, lanes] + scale[:, lanes] * lifted[i] for i in range(3)]
         for i in range(3):
             velocity_out[i, :, lanes] = now[i]
         if traces is not None:
-            vel_traces(traces, lanes, now, stage)
-
-
-def call(name, kernel, args, outs, specs=None, cost=0, scratch=()):
+            vel_traces(traces, values, lanes, now, stage)
+        if finish is not None:
+            finish(lanes)
+
+
+def call(name, kernel, args, outs, specs=None, cost=0, scratch=(), out_specs=None):
     whole = pl.BlockSpec(memory_space=pltpu.VMEM)
     specs = specs or {}
     return pl.pallas_call(
         kernel,
         name=name,
         in_specs=[specs.get(k, whole) for k in range(len(args))],
-        out_specs=[whole] * len(outs),
+        out_specs=out_specs or [whole] * len(outs),
         out_shape=[jax.ShapeDtypeStruct(s, d) for s, d in outs],
         scratch_shapes=list(scratch),
         compiler_params=pltpu.CompilerParams(vmem_limit_bytes=VMEM_LIMIT),
@@ -582,7 +610,7 @@
     three = ((shares, 3, 64 // shares, width), f32)
     trace = ((576, width), bf16)
     hot = ((6, CHUNK, width), bf16)
-    sends = [((48, HALO), f32)] * 2
+    sends = [((SEND_ROWS, 128), f32)] * 2
     lists = [((6, width), jnp.int32), ((width, 2 * MAIN), bf16),
              ((1, 2 * MAIN), jnp.int32), ((1, 2 * TAIL), jnp.int32)]
 
@@ -608,18 +636,18 @@
             args += [hots, forward] + ([rho_total] if n > 1 else [])
             outs += [field]
         else:
-            outs += [hot]
-        stress, jump, more = call(
+            outs += [hot, field, field]
+        stress, jump, *more = call(
             "vel_local", functools.partial(vel_local_kernel, n - 1), args, outs, cost=4_000_000_000,
             scratch=[nodal],
         )
         if n:
-            rho_total = more
+            rho_total, = more
         else:
-            hots = more
+            hots, lame_scaled, shear_scaled = more
         stress, jump, traces, *sent = call(
             "vel_halo", vel_halo_kernel,
-            (stress, jump, *recv, keys, hots, picks, faces, late, lame_lambda, shear_modulus),
+            (stress, jump, *recv, keys, hots, picks, faces, late, lame_scaled, shear_scaled),
             [tensor, vector, trace] + sends, scratch=[values, nodal, nodal],
         )
         recv = swap(sent, "dom")
@@ -627,22 +655,31 @@
                 forward, table["div"], table["fwd"]]
         if n:
             args += [other_total]
-        velocity, other_total = call(
-            "str_local", functools.partial(str_local_kernel, n), args, [vector, two],
-            cost=4_000_000_000, scratch=[nodal],
-        )
+        velocity, other_total, *more = call(
+            "str_local", functools.partial(str_local_kernel, n), args,
+            [vector, two] + ([] if n else [field]), cost=4_000_000_000, scratch=[nodal],
+        )
+        if not n:
+            scale, = more
         if n < steps - 1:
             velocity, traces, *sent = call(
                 "str_halo", str_halo_kernel,
-                (velocity, *recv, keys, hots, picks, faces, late, density),
+                (velocity, *recv, keys, hots, picks, faces, late, scale),
                 [vector, trace] + sends, scratch=[values, nodal, nodal],
             )
         else:
             velocity, kernel_total = call(
                 "last", functools.partial(last_kernel, n),
-                (velocity, *recv, keys, hots, density, forward, other_total)
+                (velocity, *recv, keys, hots, scale, forward, other_total)
                 + ((rho_total,) if n else ()),
-                [vector, three], scratch=[nodal],
+                [vector, three],
+                scratch=[
+                    nodal, pltpu.VMEM((3, 64, width), f32),
+                    pltpu.SemaphoreType.DMA((width // CHUNK,)),
+                ],
+                out_specs=[
+                    pl.BlockSpec(memory_space=pl.ANY), pl.BlockSpec(memory_space=pltpu.VMEM)
+                ],
             )
 
     if shares == count:

time: 76.3 us -> 75.3 us (0.987)
  no operation moved by 1% of the time
where the time goes in v1:
time: 75.3 us; the launch traced here: 75 us
  Pallas kernels  26.6 us (35%)
  starting transfers between devices  24.9 us (33%)
  blocking collectives  22.5 us (30%)
  between operations  0.95 us (1%)
    pallas_call x14, Pallas kernels, call(): pl.pallas_call(kernel, name=name, in_specs=[specs.get(k, whole) for k in...  26.6 us
    ppermute x12, starting transfers between devices, swap(): got.append(lax.ppermute(value, axis, pairs))  24.9 us
    all_to_all x1, blocking collectives, local(): parts = lax.all_to_all(kernel_total, 'event', 0, 0, tiled=True)  22.5 us
  transfers between devices with their start and end apart: 12, of which 0 were waited for; matrix products, arithmetic and copies ran while one was open for 0% of the time, Pallas kernels for 14%

profile of v1, /device:TPU:0, one launch (start us, length us, event | category | flops | bytes accessed | tf_op | source)
XLA Modules:
  0.0 75.0 jit_solution(15930004444325540517)
XLA Ops:
  0.6 0.0 copy-start.5
  0.6 0.0 copy-start.2
  0.7 0.0 copy-start.1
  0.7 2.5 %start.1 = (f32[3,64,768]{2,1,0:T(8,128)S(1)}, f32[6,64,768]{2,1,0:T(8,128)S(1)}, s32[6,768]{1,0:T(8,128)S(1)}, bf16[768,768]{1,0:T(8,128)(2,1)S(1)}, s32[1,768]...) custom-call(s32[1]{0:T(128)} %bitcast.even, ...), custom_call_target="tpu_custom_call" | custom-call | bytes 6000000 | tf_op jit(solution)/shard_map/start/pallas_call | solution.py:569
  3.2 0.7 collective-permute-start
  3.8 4.4 %collective-permute-start.1 = (f32[168,128]{1,0:T(8,128)S(1)}, f32[168,128]{1,0:T(8,128)S(1)}, u32[]{:S(2)}, u32[]{:S(2)}) collective-permute-start(f32[168,128]{1,0:T(8,128)S(1)} %get-tuple-element.61), channel_id=1, source_target_pairs={{0,8},{8,0},{16,24},{24,16},{1,9},{9,1},{17,25},{25,17},{2,10},{10... | collective-permute-start | bytes 258056 | tf_op jit(solution)/shard_map/ppermute | solution.py:588
  8.2 0.0 copy-done.5
  8.2 0.0 copy-done.2
  8.2 0.0 copy-done.1
  8.2 1.8 %vel_local.3 = (f32[6,64,768]{2,1,0:T(8,128)S(1)}, f32[3,64,768]{2,1,0:T(8,128)S(1)}, bf16[6,256,768]{2,1,0:T(8,128)(2,1)S(1)}, f32[64,768]{1,0:T(8,128)S(1)}, f32[64,768]{1,0:T(8,128)S(1)}) custom-call(f32[3,64,768]{2,1,0:T(8,128)S(1)} %get-tuple-element.54.velocity, f32[6,64,768]{2,1,0:T(8,128)S(1)} %get-tuple-element.55.stress, ...), custom_call_target="tpu_custom_call" | custom-call | flops 4000000000 | bytes 6000000 | tf_op jit(solution)/shard_map/vel_local/pallas_call | solution.py:569
  10.0 0.0 collective-permute-done.recv_one
  10.0 0.0 collective-permute-done.1.recv_two
  10.0 0.0 copy-start
  10.1 0.0 copy-start.3
  10.1 0.0 copy-start.4
  10.1 0.0 copy-start.6
  10.1 2.2 %vel_halo.3 = (f32[6,64,768]{2,1,0:T(8,128)S(1)}, f32[3,64,768]{2,1,0:T(8,128)S(1)}, bf16[576,768]{1,0:T(8,128)(2,1)S(1)}, f32[168,128]{1,0:T(8,128)S(1)}, f32[168,128]{1,0:T(8,128)S(1)}) custom-call(f32[6,64,768]{2,1,0:T(8,128)S(1)} %get-tuple-element.58.stress, f32[3,64,768]{2,1,0:T(8,128)S(1)} %get-tuple-element.59.jump, ...), custom_call_target="tpu_custom_call" | custom-call | bytes 6000000 | tf_op jit(solution)/shard_map/vel_halo/pallas_call | solution.py:569
  12.3 0.7 collective-permute-start.2
  13.0 3.3 %collective-permute-start.3 = (f32[168,128]{1,0:T(8,128)S(1)}, f32[168,128]{1,0:T(8,128)S(1)}, u32[]{:S(2)}, u32[]{:S(2)}) collective-permute-start(f32[168,128]{1,0:T(8,128)S(1)} %get-tuple-element.73), channel_id=1, source_target_pairs={{0,8},{8,0},{16,24},{24,16},{1,9},{9,1},{17,25},{25,17},{2,10},{10... | collective-permute-start | bytes 258056 | tf_op jit(solution)/shard_map/ppermute | solution.py:588
  16.3 0.0 copy-done
  16.3 0.0 copy-done.3
  16.3 0.0 copy-done.4
  16.3 0.0 copy-done.6
  16.3 1.9 %str_local.3 = (f32[3,64,768]{2,1,0:T(8,128)S(1)}, f32[8,2,8,768]{3,2,1,0:T(8,128)S(1)}, f32[64,768]{1,0:T(8,128)S(1)}) custom-call(f32[3,64,768]{2,1,0:T(8,128)S(1)} %get-tuple-element.54.velocity, f32[6,64,768]{2,1,0:T(8,128)S(1)} %get-tuple-element.68.stress, f32[3,64,768]{2,1,0:T(8,128)S(1)} %get-tuple-element.69.jump, ...), custom_call_target="tpu_custom_call" | custom-call | flops 4000000000 | bytes 6000000 | tf_op jit(solution)/shard_map/str_local/pallas_call | solution.py:569
  18.2 0.0 collective-permute-done.2.recv_one
  18.3 0.0 collective-permute-done.3.recv_two
  18.3 2.0 %str_halo.2 = (f32[3,64,768]{2,1,0:T(8,128)S(1)}, bf16[576,768]{1,0:T(8,128)(2,1)S(1)}, f32[168,128]{1,0:T(8,128)S(1)}, f32[168,128]{1,0:T(8,128)S(1)}) custom-call(f32[3,64,768]{2,1,0:T(8,128)S(1)} %get-tuple-element.71.velocity, f32[168,128]{1,0:T(8,128)S(1)} %collective-permute-done.2.recv_one, f32[168,128]{1,0:T(8,128)S(1)} %collective-permute-done.3.recv_two, ...), custom_call_target="tpu_custom_call" | custom-call | bytes 6000000 | tf_op jit(solution)/shard_map/str_halo/pallas_call | solution.py:569
  20.3 0.7 collective-permute-start.4
  21.0 3.2 %collective-permute-start.5 = (f32[168,128]{1,0:T(8,128)S(1)}, f32[168,128]{1,0:T(8,128)S(1)}, u32[]{:S(2)}, u32[]{:S(2)}) collective-permute-start(f32[168,128]{1,0:T(8,128)S(1)} %get-tuple-element.80), channel_id=1, source_target_pairs={{0,8},{8,0},{16,24},{24,16},{1,9},{9,1},{17,25},{25,17},{2,10},{10... | collective-permute-start | bytes 258056 | tf_op jit(solution)/shard_map/ppermute | solution.py:588
  24.1 1.6 %vel_local.4 = (f32[6,64,768]{2,1,0:T(8,128)S(1)}, f32[3,64,768]{2,1,0:T(8,128)S(1)}, f32[64,768]{1,0:T(8,128)S(1)}) custom-call(f32[3,64,768]{2,1,0:T(8,128)S(1)} %get-tuple-element.75.velocity, f32[6,64,768]{2,1,0:T(8,128)S(1)} %get-tuple-element.68.stress, bf16[576,768]{1,0:T(8,128)(2,1)S(1)} %get-tuple-element.76.traces, ...), custom_call_target="tpu_custom_call" | custom-call | flops 4000000000 | bytes 6000000 | tf_op jit(solution)/shard_map/vel_local/pallas_call | solution.py:569
  25.8 0.0 collective-permute-done.4.recv_one
  25.8 0.0 collective-permute-done.5.recv_two
  25.8 2.2 %vel_halo.4 = (f32[6,64,768]{2,1,0:T(8,128)S(1)}, f32[3,64,768]{2,1,0:T(8,128)S(1)}, bf16[576,768]{1,0:T(8,128)(2,1)S(1)}, f32[168,128]{1,0:T(8,128)S(1)}, f32[168,128]{1,0:T(8,128)S(1)}) custom-call(f32[6,64,768]{2,1,0:T(8,128)S(1)} %get-tuple-element.77.stress, f32[3,64,768]{2,1,0:T(8,128)S(1)} %get-tuple-element.78.jump, ...), custom_call_target="tpu_custom_call" | custom-call | bytes 6000000 | tf_op jit(solution)/shard_map/vel_halo/pallas_call | solution.py:569
  28.0 0.8 %collective-permute-start.6 = (f32[168,128]{1,0:T(8,128)S(1)}, f32[168,128]{1,0:T(8,128)S(1)}, u32[]{:S(2)}, u32[]{:S(2)}) collective-permute-start(f32[168,128]{1,0:T(8,128)S(1)} %get-tuple-element.86), channel_id=1, source_target_pairs={{8,16},{16,8},{9,17},{17,9},{10,18},{18,10},{11,19},{19,11},{12,20... | collective-permute-start | bytes 258056 | tf_op jit(solution)/shard_map/ppermute | solution.py:588
  28.9 3.5 %collective-permute-start.7 = (f32[168,128]{1,0:T(8,128)S(1)}, f32[168,128]{1,0:T(8,128)S(1)}, u32[]{:S(2)}, u32[]{:S(2)}) collective-permute-start(f32[168,128]{1,0:T(8,128)S(1)} %get-tuple-element.87), channel_id=1, source_target_pairs={{0,8},{8,0},{16,24},{24,16},{1,9},{9,1},{17,25},{25,17},{2,10},{10... | collective-permute-start | bytes 258056 | tf_op jit(solution)/shard_map/ppermute | solution.py:588
  32.3 1.9 %str_local.4 = (f32[3,64,768]{2,1,0:T(8,128)S(1)}, f32[8,2,8,768]{3,2,1,0:T(8,128)S(1)}) custom-call(f32[3,64,768]{2,1,0:T(8,128)S(1)} %get-tuple-element.75.velocity, f32[6,64,768]{2,1,0:T(8,128)S(1)} %get-tuple-element.81.stress, f32[3,64,768]{2,1,0:T(8,128)S(1)} %get-tuple-element.82.jump, bf16[576,768]{1,0:T(8,128)(2,1)S(1)} %get-tuple-element.83.traces, ...), custom_call_target="tpu_custom_call" | custom-call | flops 4000000000 | bytes 6000000 | tf_op jit(solution)/shard_map/str_local/pallas_call | solution.py:569
  34.3 0.0 collective-permute-done.6.recv_one
  34.3 0.0 collective-permute-done.7.recv_two
  34.3 2.0 %str_halo.3 = (f32[3,64,768]{2,1,0:T(8,128)S(1)}, bf16[576,768]{1,0:T(8,128)(2,1)S(1)}, f32[168,128]{1,0:T(8,128)S(1)}, f32[168,128]{1,0:T(8,128)S(1)}) custom-call(f32[3,64,768]{2,1,0:T(8,128)S(1)} %get-tuple-element.85.velocity, f32[168,128]{1,0:T(8,128)S(1)} %collective-permute-done.6.recv_one, f32[168,128]{1,0:T(8,128)S(1)} %collective-permute-done.7.recv_two, ...), custom_call_target="tpu_custom_call" | custom-call | bytes 6000000 | tf_op jit(solution)/shard_map/str_halo/pallas_call | solution.py:569
  36.3 0.7 collective-permute-start.8
  37.0 3.0 %collective-permute-start.9 = (f32[168,128]{1,0:T(8,128)S(1)}, f32[168,128]{1,0:T(8,128)S(1)}, u32[]{:S(2)}, u32[]{:S(2)}) collective-permute-start(f32[168,128]{1,0:T(8,128)S(1)} %get-tuple-element.94), channel_id=1, source_target_pairs={{0,8},{8,0},{16,24},{24,16},{1,9},{9,1},{17,25},{25,17},{2,10},{10... | collective-permute-start | bytes 258056 | tf_op jit(solution)/shard_map/ppermute | solution.py:588
  40.0 1.7 %vel_local.5 = (f32[6,64,768]{2,1,0:T(8,128)S(1)}, f32[3,64,768]{2,1,0:T(8,128)S(1)}, f32[64,768]{1,0:T(8,128)S(1)}) custom-call(f32[3,64,768]{2,1,0:T(8,128)S(1)} %get-tuple-element.88.velocity, f32[6,64,768]{2,1,0:T(8,128)S(1)} %get-tuple-element.81.stress, bf16[576,768]{1,0:T(8,128)(2,1)S(1)} %get-tuple-element.89.traces, ...), custom_call_target="tpu_custom_call" | custom-call | flops 4000000000 | bytes 6000000 | tf_op jit(solution)/shard_map/vel_local/pallas_call | solution.py:569
  41.7 0.0 collective-permute-done.8.recv_one
  41.7 0.0 collective-permute-done.9.recv_two
  41.7 2.2 %vel_halo.5 = (f32[6,64,768]{2,1,0:T(8,128)S(1)}, f32[3,64,768]{2,1,0:T(8,128)S(1)}, bf16[576,768]{1,0:T(8,128)(2,1)S(1)}, f32[168,128]{1,0:T(8,128)S(1)}, f32[168,128]{1,0:T(8,128)S(1)}) custom-call(f32[6,64,768]{2,1,0:T(8,128)S(1)} %get-tuple-element.91.stress, f32[3,64,768]{2,1,0:T(8,128)S(1)} %get-tuple-element.92.jump, ...), custom_call_target="tpu_custom_call" | custom-call | bytes 6000000 | tf_op jit(solution)/shard_map/vel_halo/pallas_call | solution.py:569
  43.9 0.7 collective-permute-start.10
  44.6 3.4 %collective-permute-start.11 = (f32[168,128]{1,0:T(8,128)S(1)}, f32[168,128]{1,0:T(8,128)S(1)}, u32[]{:S(2)}, u32[]{:S(2)}) collective-permute-start(f32[168,128]{1,0:T(8,128)S(1)} %get-tuple-element.101), channel_id=1, source_target_pairs={{0,8},{8,0},{16,24},{24,16},{1,9},{9,1},{17,25},{25,17},{2,10},{10... | collective-permute-start | bytes 258056 | tf_op jit(solution)/shard_map/ppermute | solution.py:588
  48.0 1.9 %str_local.5 = (f32[3,64,768]{2,1,0:T(8,128)S(1)}, f32[8,2,8,768]{3,2,1,0:T(8,128)S(1)}) custom-call(f32[3,64,768]{2,1,0:T(8,128)S(1)} %get-tuple-element.88.velocity, f32[6,64,768]{2,1,0:T(8,128)S(1)} %get-tuple-element.95.stress, f32[3,64,768]{2,1,0:T(8,128)S(1)} %get-tuple-element.96.jump, bf16[576,768]{1,0:T(8,128)(2,1)S(1)} %get-tuple-element.97.traces, ...), custom_call_target="tpu_custom_call" | custom-call | flops 4000000000 | bytes 6000000 | tf_op jit(solution)/shard_map/str_local/pallas_call | solution.py:569
  49.9 0.0 collective-permute-done.10.recv_one
  49.9 0.0 collective-permute-done.11.recv_two
  49.9 1.8 %last.1 = (f32[3,64,768]{2,1,0:T(8,128)}, f32[8,3,8,768]{3,2,1,0:T(8,128)S(1)}) custom-call(f32[3,64,768]{2,1,0:T(8,128)S(1)} %get-tuple-element.99.velocity, f32[168,128]{1,0:T(8,128)S(1)} %collective-permute-done.10.recv_one, f32[168,128]{1,0:T(8,128)S(1)} %collective-permute-done.11.recv_two, s32[6,768]{1,0:T(8,128)S(1)} %get-tuple-element.57.keys, ...), custom_call_target="tpu_custom_call" | custom-call | bytes 6000000 | tf_op jit(solution)/shard_map/last/pallas_call | solution.py:569
  51.8 22.5 %all_to_all.5.parts = f32[8,3,8,768]{3,2,1,0:T(8,128)S(1)} all-to-all(f32[8,3,8,768]{3,2,1,0:T(8,128)S(1)} %get-tuple-element.105), channel_id=1, replica_groups=mesh['dom'=4,'event'=8] {'event'}, dimensions={0} | all-to-all | bytes 1179648 | tf_op jit(solution)/shard_map/all_to_all | solution.py:686
  74.3 0.7 event_sum.1
Async XLA Ops:
  0.6 7.6 %copy-start.5 = (bf16[192,192]{1,0:T(8,128)(2,1)S(1)}, bf16[192,192]{1,0:T(8,128)(2,1)}, u32[]{:S(2)}) copy-start(bf16[192,192]{1,0:T(8,128)(2,1)} %constant.25.clone.vel) | copy-start | bytes 221188
  0.6 7.6 %copy-start.2 = (f32[64,768]{1,0:T(8,128)S(1)}, f32[64,768]{1,0:T(8,128)}, u32[]{:S(2)}) copy-start(f32[64,768]{1,0:T(8,128)} %shear.11) | copy-start | bytes 589828
  0.7 7.6 %copy-start.1 = (f32[64,768]{1,0:T(8,128)S(1)}, f32[64,768]{1,0:T(8,128)}, u32[]{:S(2)}) copy-start(f32[64,768]{1,0:T(8,128)} %lame.11) | copy-start | bytes 589828
  3.2 6.9 %collective-permute-start = (f32[168,128]{1,0:T(8,128)S(1)}, f32[168,128]{1,0:T(8,128)S(1)}, u32[]{:S(2)}, u32[]{:S(2)}) collective-permute-start(f32[168,128]{1,0:T(8,128)S(1)} %get-tuple-element.60), channel_id=1, source_target_pairs={{8,16},{16,8},{9,17},{17,9},{10,18},{18,10},{11,19},{19,11},{12,20... | collective-permute-start | bytes 258056 | tf_op jit(solution)/shard_map/ppermute | solution.py:588
  3.8 6.2 %collective-permute-start.1 = (f32[168,128]{1,0:T(8,128)S(1)}, f32[168,128]{1,0:T(8,128)S(1)}, u32[]{:S(2)}, u32[]{:S(2)}) collective-permute-start(f32[168,128]{1,0:T(8,128)S(1)} %get-tuple-element.61), channel_id=1, source_target_pairs={{0,8},{8,0},{16,24},{24,16},{1,9},{9,1},{17,25},{25,17},{2,10},{10... | collective-permute-start | bytes 258056 | tf_op jit(solution)/shard_map/ppermute | solution.py:588
  10.0 6.2 %copy-start = (f32[1,3,3,64,768]{4,3,2,1,0:T(8,128)S(1)}, f32[1,3,3,64,768]{4,3,2,1,0:T(8,128)}, u32[]{:S(2)}) copy-start(f32[1,3,3,64,768]{4,3,2,1,0:T(8,128)} %param.11) | copy-start | bytes 5308420
  10.1 6.2 %copy-start.3 = (f32[64,768]{1,0:T(8,128)S(1)}, f32[64,768]{1,0:T(8,128)}, u32[]{:S(2)}) copy-start(f32[64,768]{1,0:T(8,128)} %density.5) | copy-start | bytes 589828
  10.1 6.2 %copy-start.4 = (bf16[192,192]{1,0:T(8,128)(2,1)S(1)}, bf16[192,192]{1,0:T(8,128)(2,1)}, u32[]{:S(2)}) copy-start(bf16[192,192]{1,0:T(8,128)(2,1)} %constant.26.clone.fwd) | copy-start | bytes 221188
  10.1 6.2 %copy-start.6 = (bf16[64,576]{1,0:T(8,128)(2,1)S(1)}, bf16[64,576]{1,0:T(8,128)(2,1)}, u32[]{:S(2)}) copy-start(bf16[64,576]{1,0:T(8,128)(2,1)} %constant.27.clone.div) | copy-start | bytes 221188
  12.3 5.9 %collective-permute-start.2 = (f32[168,128]{1,0:T(8,128)S(1)}, f32[168,128]{1,0:T(8,128)S(1)}, u32[]{:S(2)}, u32[]{:S(2)}) collective-permute-start(f32[168,128]{1,0:T(8,128)S(1)} %get-tuple-element.72), channel_id=1, source_target_pairs={{8,16},{16,8},{9,17},{17,9},{10,18},{18,10},{11,19},{19,11},{12,20... | collective-permute-start | bytes 258056 | tf_op jit(solution)/shard_map/ppermute | solution.py:588
  13.0 5.3 %collective-permute-start.3 = (f32[168,128]{1,0:T(8,128)S(1)}, f32[168,128]{1,0:T(8,128)S(1)}, u32[]{:S(2)}, u32[]{:S(2)}) collective-permute-start(f32[168,128]{1,0:T(8,128)S(1)} %get-tuple-element.73), channel_id=1, source_target_pairs={{0,8},{8,0},{16,24},{24,16},{1,9},{9,1},{17,25},{25,17},{2,10},{10... | collective-permute-start | bytes 258056 | tf_op jit(solution)/shard_map/ppermute | solution.py:588
  20.3 5.5 %collective-permute-start.4 = (f32[168,128]{1,0:T(8,128)S(1)}, f32[168,128]{1,0:T(8,128)S(1)}, u32[]{:S(2)}, u32[]{:S(2)}) collective-permute-start(f32[168,128]{1,0:T(8,128)S(1)} %get-tuple-element.79), channel_id=1, source_target_pairs={{8,16},{16,8},{9,17},{17,9},{10,18},{18,10},{11,19},{19,11},{12,20... | collective-permute-start | bytes 258056 | tf_op jit(solution)/shard_map/ppermute | solution.py:588
  21.0 4.8 %collective-permute-start.5 = (f32[168,128]{1,0:T(8,128)S(1)}, f32[168,128]{1,0:T(8,128)S(1)}, u32[]{:S(2)}, u32[]{:S(2)}) collective-permute-start(f32[168,128]{1,0:T(8,128)S(1)} %get-tuple-element.80), channel_id=1, source_target_pairs={{0,8},{8,0},{16,24},{24,16},{1,9},{9,1},{17,25},{25,17},{2,10},{10... | collective-permute-start | bytes 258056 | tf_op jit(solution)/shard_map/ppermute | solution.py:588
  28.0 6.2 %collective-permute-start.6 = (f32[168,128]{1,0:T(8,128)S(1)}, f32[168,128]{1,0:T(8,128)S(1)}, u32[]{:S(2)}, u32[]{:S(2)}) collective-permute-start(f32[168,128]{1,0:T(8,128)S(1)} %get-tuple-element.86), channel_id=1, source_target_pairs={{8,16},{16,8},{9,17},{17,9},{10,18},{18,10},{11,19},{19,11},{12,20... | collective-permute-start | bytes 258056 | tf_op jit(solution)/shard_map/ppermute | solution.py:588
  28.9 5.4 %collective-permute-start.7 = (f32[168,128]{1,0:T(8,128)S(1)}, f32[168,128]{1,0:T(8,128)S(1)}, u32[]{:S(2)}, u32[]{:S(2)}) collective-permute-start(f32[168,128]{1,0:T(8,128)S(1)} %get-tuple-element.87), channel_id=1, source_target_pairs={{0,8},{8,0},{16,24},{24,16},{1,9},{9,1},{17,25},{25,17},{2,10},{10... | collective-permute-start | bytes 258056 | tf_op jit(solution)/shard_map/ppermute | solution.py:588
  36.3 5.4 %collective-permute-start.8 = (f32[168,128]{1,0:T(8,128)S(1)}, f32[168,128]{1,0:T(8,128)S(1)}, u32[]{:S(2)}, u32[]{:S(2)}) collective-permute-start(f32[168,128]{1,0:T(8,128)S(1)} %get-tuple-element.93), channel_id=1, source_target_pairs={{8,16},{16,8},{9,17},{17,9},{10,18},{18,10},{11,19},{19,11},{12,20... | collective-permute-start | bytes 258056 | tf_op jit(solution)/shard_map/ppermute | solution.py:588
  37.0 4.7 %collective-permute-start.9 = (f32[168,128]{1,0:T(8,128)S(1)}, f32[168,128]{1,0:T(8,128)S(1)}, u32[]{:S(2)}, u32[]{:S(2)}) collective-permute-start(f32[168,128]{1,0:T(8,128)S(1)} %get-tuple-element.94), channel_id=1, source_target_pairs={{0,8},{8,0},{16,24},{24,16},{1,9},{9,1},{17,25},{25,17},{2,10},{10... | collective-permute-start | bytes 258056 | tf_op jit(solution)/shard_map/ppermute | solution.py:588
  43.9 6.0 %collective-permute-start.10 = (f32[168,128]{1,0:T(8,128)S(1)}, f32[168,128]{1,0:T(8,128)S(1)}, u32[]{:S(2)}, u32[]{:S(2)}) collective-permute-start(f32[168,128]{1,0:T(8,128)S(1)} %get-tuple-element.100), channel_id=1, source_target_pairs={{8,16},{16,8},{9,17},{17,9},{10,18},{18,10},{11,19},{19,11},{12,20... | collective-permute-start | bytes 258056 | tf_op jit(solution)/shard_map/ppermute | solution.py:588
  44.6 5.3 %collective-permute-start.11 = (f32[168,128]{1,0:T(8,128)S(1)}, f32[168,128]{1,0:T(8,128)S(1)}, u32[]{:S(2)}, u32[]{:S(2)}) collective-permute-start(f32[168,128]{1,0:T(8,128)S(1)} %get-tuple-element.101), channel_id=1, source_target_pairs={{0,8},{8,0},{16,24},{24,16},{1,9},{9,1},{17,25},{25,17},{2,10},{10... | collective-permute-start | bytes 258056 | tf_op jit(solution)/shard_map/ppermute | solution.py:588

commit v2 on v1

--- a/solution.py
+++ b/solution.py
@@ -15,9 +15,10 @@
 f32 = jnp.float32
 bf16 = jnp.bfloat16
 CHUNK = 256
-MAIN = 384
+MAIN = 256
+MID = 128
 TAIL = 64
-SEND_MAIN = 48 * MAIN // 128
+SEND_MAIN = 48 * (MAIN + MID) // 128
 SEND_ROWS = SEND_MAIN + 48 * TAIL // 128
 VMEM_LIMIT = 40 * 2**20
 
@@ -184,18 +185,24 @@
     )
 
 
-def halo_faces(lhs, tail, keys, hots, lanes, width):
+def halo_faces(lhs, late, keys, hots, lanes, width):
     blocks = 2 * MAIN // CHUNK
     first = width // CHUNK
+    late_first = (width + 2 * MAIN) // 128
     out = []
     for f in range(6):
         key = keys[f:f + 1]
         got = mm(lhs, hots[f, :, lanes])
+        parts = []
+        for at in range(0, CHUNK, 128):
+            lane = key[:, at:at + 128] & 127
+            tile = key[:, at:at + 128] >> 7
+            part = jnp.zeros((48, 128), f32)
+            for t, source in enumerate(late):
+                part = jnp.where(tile == late_first + t, gather_tile(source, lane), part)
+            parts.append(part)
+        total = jnp.concatenate(parts, axis=1)
         which = key >> 8
-        late = jnp.concatenate(
-            [gather_tile(tail, key[:, t:t + 128] & 127) for t in range(0, CHUNK, 128)], axis=1
-        )
-        total = jnp.where(which == first + blocks, late, 0.0)
         for a in range(blocks):
             both = got[48 * a:48 * a + 48] + got[48 * (blocks + a):48 * (blocks + a) + 48]
             total = jnp.where(which == first + a, both, total)
@@ -217,7 +224,8 @@
         ],
         axis=0,
     )
-    return jnp.concatenate([high, low], axis=0), tail
+    mid = [recv[SEND_MAIN - 48:SEND_MAIN] for recv in (recv_one, recv_two)]
+    return jnp.concatenate([high, low], axis=0), [*mid, tail]
 
 
 def local_faces(traces, keys, hots, lanes, own_sign):
@@ -279,15 +287,21 @@
     for t in range(MAIN // 128):
         for first, send in ((0, send_one), (MAIN, send_two)):
             send[48 * t:48 * t + 48] = whole[:, first + 128 * t:first + 128 * t + 128]
-    key = late[...]
-    lane = key & 127
-    which = jnp.broadcast_to(key >> 7, (48, 128))
-    total = jnp.zeros((48, 128), f32)
-    for f in range(6):
-        for a in range(width // 128):
-            got = gather_tile(values[48 * f:48 * f + 48, 128 * a:128 * a + 128], lane)
-            total = jnp.where(which == f * (width // 128) + a, got, total)
-    one, two = total[:, 0:TAIL], total[:, TAIL:2 * TAIL]
+    tiles = width // 128
+    rest = []
+    for s in (slice(t, t + 128) for t in range(0, late.shape[1], 128)):
+        key = late[:, s]
+        lane = key & 127
+        which = jnp.broadcast_to(key >> 7, (48, 128))
+        total = jnp.zeros((48, 128), f32)
+        for f in range(6):
+            for a in range(tiles):
+                got = gather_tile(values[48 * f:48 * f + 48, 128 * a:128 * a + 128], lane)
+                total = jnp.where(which == f * tiles + a, got, total)
+        rest.append(total)
+    send_one[SEND_MAIN - 48:SEND_MAIN] = rest[0]
+    send_two[SEND_MAIN - 48:SEND_MAIN] = rest[1]
+    one, two = rest[2][:, 0:TAIL], rest[2][:, TAIL:2 * TAIL]
     send_one[SEND_MAIN:SEND_ROWS] = jnp.concatenate([one[0:24], one[24:48]], axis=1)
     send_two[SEND_MAIN:SEND_ROWS] = jnp.concatenate([two[0:24], two[24:48]], axis=1)
 
@@ -345,17 +359,26 @@
     at = code - width - jnp.where(low, 0, cap)
     second = jnp.where(low == is_even, 0, 1)
     place = jnp.where(
-        at < MAIN, at + MAIN * second, at - MAIN + 2 * MAIN + TAIL * second
+        at < MAIN,
+        at + MAIN * second,
+        jnp.where(
+            at < MAIN + MID,
+            at + MAIN + MID * second,
+            at + MAIN + MID + TAIL * second,
+        ),
     )
     keys[...] = jnp.where(code < width, code, width + place)
     valid = jnp.where(jnp.max(code, axis=0, keepdims=True) >= 0, 1.0, 0.0)
     entries = send_list[...]
     entries = jnp.concatenate(
-        [entries, jnp.full((2, MAIN + TAIL - cap), -1, jnp.int32)], axis=1
+        [entries, jnp.full((2, MAIN + MID + TAIL - cap), -1, jnp.int32)], axis=1
     )
     one, two = entries[0:1], entries[1:2]
     one, two = jnp.where(is_even, one, two), jnp.where(is_even, two, one)
-    late[...] = jnp.concatenate([one[:, MAIN:], two[:, MAIN:]], axis=1)
+    late[...] = jnp.concatenate(
+        [x[:, c] for c in (slice(MAIN, MAIN + MID), slice(MAIN + MID, None)) for x in (one, two)],
+        axis=1,
+    )
     main = jnp.concatenate([one[:, 0:MAIN], two[:, 0:MAIN]], axis=1)
     face = jnp.zeros_like(main)
     for f in range(1, 6):
@@ -371,11 +394,11 @@
         for i in range(3):
             velocity[i, :, lanes] = now[i]
         vel_traces(traces, values, lanes, now, stage)
-    pack(traces, values, picks, faces, late, send_one, send_two)
     copies[3].wait()
     for lanes in chunks(width):
         for i in range(6):
             stress[i, :, lanes] = state[3 + i, :, lanes] * valid[:, lanes]
+    pack(traces, values, picks, faces, late, send_one, send_two)
 
 
 def vel_local_kernel(
@@ -612,7 +635,7 @@
     hot = ((6, CHUNK, width), bf16)
     sends = [((SEND_ROWS, 128), f32)] * 2
     lists = [((6, width), jnp.int32), ((width, 2 * MAIN), bf16),
-             ((1, 2 * MAIN), jnp.int32), ((1, 2 * TAIL), jnp.int32)]
+             ((1, 2 * MAIN), jnp.int32), ((1, 2 * MID + 2 * TAIL), jnp.int32)]
 
     velocity, stress, keys, picks, faces, late, traces, *sent = call(
         "start", start_kernel,

time: 75.3 us -> 76 us (level)
  no operation moved by 1% of the time
where the time goes in v2:
time: 76 us; the launch traced here: 75.7 us
  Pallas kernels  27.3 us (36%)
  starting transfers between devices  25.1 us (33%)
  blocking collectives  22.3 us (29%)
  between operations  0.91 us (1%)
    pallas_call x14, Pallas kernels, call(): pl.pallas_call(kernel, name=name, in_specs=[specs.get(k, whole) for k in...  27.3 us
    ppermute x12, starting transfers between devices, swap(): got.append(lax.ppermute(value, axis, pairs))  25.1 us
    all_to_all x1, blocking collectives, local(): parts = lax.all_to_all(kernel_total, 'event', 0, 0, tiled=True)  22.3 us
  transfers between devices with their start and end apart: 12, of which 0 were waited for; matrix products, arithmetic and copies ran while one was open for 0% of the time, Pallas kernels for 14%

profile of v2, /device:TPU:0, one launch (start us, length us, event | category | flops | bytes accessed | tf_op | source)
XLA Modules:
  0.0 75.7 jit_solution(6538626932189545446)
XLA Ops:
  0.6 0.0 copy-start.5
  0.6 0.0 copy-start.2
  0.7 0.0 copy-start.1
  0.7 2.5 %start.1 = (f32[3,64,768]{2,1,0:T(8,128)S(1)}, f32[6,64,768]{2,1,0:T(8,128)S(1)}, s32[6,768]{1,0:T(8,128)S(1)}, bf16[768,512]{1,0:T(8,128)(2,1)S(1)}, s32[1,512]...) custom-call(s32[1]{0:T(128)} %bitcast.even, ...), custom_call_target="tpu_custom_call" | custom-call | bytes 6000000 | tf_op jit(solution)/shard_map/start/pallas_call | solution.py:592
  3.2 0.7 collective-permute-start
  3.9 4.4 %collective-permute-start.1 = (f32[168,128]{1,0:T(8,128)S(1)}, f32[168,128]{1,0:T(8,128)S(1)}, u32[]{:S(2)}, u32[]{:S(2)}) collective-permute-start(f32[168,128]{1,0:T(8,128)S(1)} %get-tuple-element.61), channel_id=1, source_target_pairs={{0,8},{8,0},{16,24},{24,16},{1,9},{9,1},{17,25},{25,17},{2,10},{10... | collective-permute-start | bytes 258056 | tf_op jit(solution)/shard_map/ppermute | solution.py:611
  8.3 0.0 copy-done.5
  8.3 0.0 copy-done.2
  8.3 0.0 copy-done.1
  8.3 1.8 %vel_local.3 = (f32[6,64,768]{2,1,0:T(8,128)S(1)}, f32[3,64,768]{2,1,0:T(8,128)S(1)}, bf16[6,256,768]{2,1,0:T(8,128)(2,1)S(1)}, f32[64,768]{1,0:T(8,128)S(1)}, f32[64,768]{1,0:T(8,128)S(1)}) custom-call(f32[3,64,768]{2,1,0:T(8,128)S(1)} %get-tuple-element.54.velocity, f32[6,64,768]{2,1,0:T(8,128)S(1)} %get-tuple-element.55.stress, ...), custom_call_target="tpu_custom_call" | custom-call | flops 4000000000 | bytes 6000000 | tf_op jit(solution)/shard_map/vel_local/pallas_call | solution.py:592
  10.1 0.0 collective-permute-done.recv_one
  10.1 0.0 collective-permute-done.1.recv_two
  10.1 0.0 copy-start
  10.1 0.0 copy-start.3
  10.1 0.0 copy-start.4
  10.1 0.0 copy-start.6
  10.2 2.3 %vel_halo.3 = (f32[6,64,768]{2,1,0:T(8,128)S(1)}, f32[3,64,768]{2,1,0:T(8,128)S(1)}, bf16[576,768]{1,0:T(8,128)(2,1)S(1)}, f32[168,128]{1,0:T(8,128)S(1)}, f32[168,128]{1,0:T(8,128)S(1)}) custom-call(f32[6,64,768]{2,1,0:T(8,128)S(1)} %get-tuple-element.58.stress, f32[3,64,768]{2,1,0:T(8,128)S(1)} %get-tuple-element.59.jump, ...), custom_call_target="tpu_custom_call" | custom-call | bytes 6000000 | tf_op jit(solution)/shard_map/vel_halo/pallas_call | solution.py:592
  12.5 0.7 collective-permute-start.2
  13.1 3.3 %collective-permute-start.3 = (f32[168,128]{1,0:T(8,128)S(1)}, f32[168,128]{1,0:T(8,128)S(1)}, u32[]{:S(2)}, u32[]{:S(2)}) collective-permute-start(f32[168,128]{1,0:T(8,128)S(1)} %get-tuple-element.73), channel_id=1, source_target_pairs={{0,8},{8,0},{16,24},{24,16},{1,9},{9,1},{17,25},{25,17},{2,10},{10... | collective-permute-start | bytes 258056 | tf_op jit(solution)/shard_map/ppermute | solution.py:611
  16.4 0.0 copy-done
  16.4 0.0 copy-done.3
  16.4 0.0 copy-done.4
  16.4 0.0 copy-done.6
  16.4 1.9 %str_local.3 = (f32[3,64,768]{2,1,0:T(8,128)S(1)}, f32[8,2,8,768]{3,2,1,0:T(8,128)S(1)}, f32[64,768]{1,0:T(8,128)S(1)}) custom-call(f32[3,64,768]{2,1,0:T(8,128)S(1)} %get-tuple-element.54.velocity, f32[6,64,768]{2,1,0:T(8,128)S(1)} %get-tuple-element.68.stress, f32[3,64,768]{2,1,0:T(8,128)S(1)} %get-tuple-element.69.jump, ...), custom_call_target="tpu_custom_call" | custom-call | flops 4000000000 | bytes 6000000 | tf_op jit(solution)/shard_map/str_local/pallas_call | solution.py:592
  18.4 0.0 collective-permute-done.2.recv_one
  18.4 0.0 collective-permute-done.3.recv_two
  18.4 2.1 %str_halo.2 = (f32[3,64,768]{2,1,0:T(8,128)S(1)}, bf16[576,768]{1,0:T(8,128)(2,1)S(1)}, f32[168,128]{1,0:T(8,128)S(1)}, f32[168,128]{1,0:T(8,128)S(1)}) custom-call(f32[3,64,768]{2,1,0:T(8,128)S(1)} %get-tuple-element.71.velocity, f32[168,128]{1,0:T(8,128)S(1)} %collective-permute-done.2.recv_one, f32[168,128]{1,0:T(8,128)S(1)} %collective-permute-done.3.recv_two, ...), custom_call_target="tpu_custom_call" | custom-call | bytes 6000000 | tf_op jit(solution)/shard_map/str_halo/pallas_call | solution.py:592
  20.6 0.8 %collective-permute-start.4 = (f32[168,128]{1,0:T(8,128)S(1)}, f32[168,128]{1,0:T(8,128)S(1)}, u32[]{:S(2)}, u32[]{:S(2)}) collective-permute-start(f32[168,128]{1,0:T(8,128)S(1)} %get-tuple-element.79), channel_id=1, source_target_pairs={{8,16},{16,8},{9,17},{17,9},{10,18},{18,10},{11,19},{19,11},{12,20... | collective-permute-start | bytes 258056 | tf_op jit(solution)/shard_map/ppermute | solution.py:611
  21.4 3.2 %collective-permute-start.5 = (f32[168,128]{1,0:T(8,128)S(1)}, f32[168,128]{1,0:T(8,128)S(1)}, u32[]{:S(2)}, u32[]{:S(2)}) collective-permute-start(f32[168,128]{1,0:T(8,128)S(1)} %get-tuple-element.80), channel_id=1, source_target_pairs={{0,8},{8,0},{16,24},{24,16},{1,9},{9,1},{17,25},{25,17},{2,10},{10... | collective-permute-start | bytes 258056 | tf_op jit(solution)/shard_map/ppermute | solution.py:611
  24.6 1.6 %vel_local.4 = (f32[6,64,768]{2,1,0:T(8,128)S(1)}, f32[3,64,768]{2,1,0:T(8,128)S(1)}, f32[64,768]{1,0:T(8,128)S(1)}) custom-call(f32[3,64,768]{2,1,0:T(8,128)S(1)} %get-tuple-element.75.velocity, f32[6,64,768]{2,1,0:T(8,128)S(1)} %get-tuple-element.68.stress, bf16[576,768]{1,0:T(8,128)(2,1)S(1)} %get-tuple-element.76.traces, ...), custom_call_target="tpu_custom_call" | custom-call | flops 4000000000 | bytes 6000000 | tf_op jit(solution)/shard_map/vel_local/pallas_call | solution.py:592
  26.2 0.0 collective-permute-done.4.recv_one
  26.2 0.0 collective-permute-done.5.recv_two
  26.2 2.3 %vel_halo.4 = (f32[6,64,768]{2,1,0:T(8,128)S(1)}, f32[3,64,768]{2,1,0:T(8,128)S(1)}, bf16[576,768]{1,0:T(8,128)(2,1)S(1)}, f32[168,128]{1,0:T(8,128)S(1)}, f32[168,128]{1,0:T(8,128)S(1)}) custom-call(f32[6,64,768]{2,1,0:T(8,128)S(1)} %get-tuple-element.77.stress, f32[3,64,768]{2,1,0:T(8,128)S(1)} %get-tuple-element.78.jump, ...), custom_call_target="tpu_custom_call" | custom-call | bytes 6000000 | tf_op jit(solution)/shard_map/vel_halo/pallas_call | solution.py:592
  28.6 0.7 collective-permute-start.6
  29.2 3.3 %collective-permute-start.7 = (f32[168,128]{1,0:T(8,128)S(1)}, f32[168,128]{1,0:T(8,128)S(1)}, u32[]{:S(2)}, u32[]{:S(2)}) collective-permute-start(f32[168,128]{1,0:T(8,128)S(1)} %get-tuple-element.87), channel_id=1, source_target_pairs={{0,8},{8,0},{16,24},{24,16},{1,9},{9,1},{17,25},{25,17},{2,10},{10... | collective-permute-start | bytes 258056 | tf_op jit(solution)/shard_map/ppermute | solution.py:611
  32.5 1.9 %str_local.4 = (f32[3,64,768]{2,1,0:T(8,128)S(1)}, f32[8,2,8,768]{3,2,1,0:T(8,128)S(1)}) custom-call(f32[3,64,768]{2,1,0:T(8,128)S(1)} %get-tuple-element.75.velocity, f32[6,64,768]{2,1,0:T(8,128)S(1)} %get-tuple-element.81.stress, f32[3,64,768]{2,1,0:T(8,128)S(1)} %get-tuple-element.82.jump, bf16[576,768]{1,0:T(8,128)(2,1)S(1)} %get-tuple-element.83.traces, ...), custom_call_target="tpu_custom_call" | custom-call | flops 4000000000 | bytes 6000000 | tf_op jit(solution)/shard_map/str_local/pallas_call | solution.py:592
  34.4 0.0 collective-permute-done.6.recv_one
  34.4 0.0 collective-permute-done.7.recv_two
  34.5 2.1 %str_halo.3 = (f32[3,64,768]{2,1,0:T(8,128)S(1)}, bf16[576,768]{1,0:T(8,128)(2,1)S(1)}, f32[168,128]{1,0:T(8,128)S(1)}, f32[168,128]{1,0:T(8,128)S(1)}) custom-call(f32[3,64,768]{2,1,0:T(8,128)S(1)} %get-tuple-element.85.velocity, f32[168,128]{1,0:T(8,128)S(1)} %collective-permute-done.6.recv_one, f32[168,128]{1,0:T(8,128)S(1)} %collective-permute-done.7.recv_two, ...), custom_call_target="tpu_custom_call" | custom-call | bytes 6000000 | tf_op jit(solution)/shard_map/str_halo/pallas_call | solution.py:592
  36.6 0.7 collective-permute-start.8
  37.3 3.2 %collective-permute-start.9 = (f32[168,128]{1,0:T(8,128)S(1)}, f32[168,128]{1,0:T(8,128)S(1)}, u32[]{:S(2)}, u32[]{:S(2)}) collective-permute-start(f32[168,128]{1,0:T(8,128)S(1)} %get-tuple-element.94), channel_id=1, source_target_pairs={{0,8},{8,0},{16,24},{24,16},{1,9},{9,1},{17,25},{25,17},{2,10},{10... | collective-permute-start | bytes 258056 | tf_op jit(solution)/shard_map/ppermute | solution.py:611
  40.5 1.7 %vel_local.5 = (f32[6,64,768]{2,1,0:T(8,128)S(1)}, f32[3,64,768]{2,1,0:T(8,128)S(1)}, f32[64,768]{1,0:T(8,128)S(1)}) custom-call(f32[3,64,768]{2,1,0:T(8,128)S(1)} %get-tuple-element.88.velocity, f32[6,64,768]{2,1,0:T(8,128)S(1)} %get-tuple-element.81.stress, bf16[576,768]{1,0:T(8,128)(2,1)S(1)} %get-tuple-element.89.traces, ...), custom_call_target="tpu_custom_call" | custom-call | flops 4000000000 | bytes 6000000 | tf_op jit(solution)/shard_map/vel_local/pallas_call | solution.py:592
  42.1 0.0 collective-permute-done.8.recv_one
  42.1 0.0 collective-permute-done.9.recv_two
  42.2 2.3 %vel_halo.5 = (f32[6,64,768]{2,1,0:T(8,128)S(1)}, f32[3,64,768]{2,1,0:T(8,128)S(1)}, bf16[576,768]{1,0:T(8,128)(2,1)S(1)}, f32[168,128]{1,0:T(8,128)S(1)}, f32[168,128]{1,0:T(8,128)S(1)}) custom-call(f32[6,64,768]{2,1,0:T(8,128)S(1)} %get-tuple-element.91.stress, f32[3,64,768]{2,1,0:T(8,128)S(1)} %get-tuple-element.92.jump, ...), custom_call_target="tpu_custom_call" | custom-call | bytes 6000000 | tf_op jit(solution)/shard_map/vel_halo/pallas_call | solution.py:592
  44.5 0.9 %collective-permute-start.10 = (f32[168,128]{1,0:T(8,128)S(1)}, f32[168,128]{1,0:T(8,128)S(1)}, u32[]{:S(2)}, u32[]{:S(2)}) collective-permute-start(f32[168,128]{1,0:T(8,128)S(1)} %get-tuple-element.100), channel_id=1, source_target_pairs={{8,16},{16,8},{9,17},{17,9},{10,18},{18,10},{11,19},{19,11},{12,20... | collective-permute-start | bytes 258056 | tf_op jit(solution)/shard_map/ppermute | solution.py:611
  45.4 3.4 %collective-permute-start.11 = (f32[168,128]{1,0:T(8,128)S(1)}, f32[168,128]{1,0:T(8,128)S(1)}, u32[]{:S(2)}, u32[]{:S(2)}) collective-permute-start(f32[168,128]{1,0:T(8,128)S(1)} %get-tuple-element.101), channel_id=1, source_target_pairs={{0,8},{8,0},{16,24},{24,16},{1,9},{9,1},{17,25},{25,17},{2,10},{10... | collective-permute-start | bytes 258056 | tf_op jit(solution)/shard_map/ppermute | solution.py:611
  48.8 1.9 %str_local.5 = (f32[3,64,768]{2,1,0:T(8,128)S(1)}, f32[8,2,8,768]{3,2,1,0:T(8,128)S(1)}) custom-call(f32[3,64,768]{2,1,0:T(8,128)S(1)} %get-tuple-element.88.velocity, f32[6,64,768]{2,1,0:T(8,128)S(1)} %get-tuple-element.95.stress, f32[3,64,768]{2,1,0:T(8,128)S(1)} %get-tuple-element.96.jump, bf16[576,768]{1,0:T(8,128)(2,1)S(1)} %get-tuple-element.97.traces, ...), custom_call_target="tpu_custom_call" | custom-call | flops 4000000000 | bytes 6000000 | tf_op jit(solution)/shard_map/str_local/pallas_call | solution.py:592
  50.7 0.0 collective-permute-done.10.recv_one
  50.7 0.0 collective-permute-done.11.recv_two
  50.7 1.9 %last.1 = (f32[3,64,768]{2,1,0:T(8,128)}, f32[8,3,8,768]{3,2,1,0:T(8,128)S(1)}) custom-call(f32[3,64,768]{2,1,0:T(8,128)S(1)} %get-tuple-element.99.velocity, f32[168,128]{1,0:T(8,128)S(1)} %collective-permute-done.10.recv_one, f32[168,128]{1,0:T(8,128)S(1)} %collective-permute-done.11.recv_two, s32[6,768]{1,0:T(8,128)S(1)} %get-tuple-element.57.keys, ...), custom_call_target="tpu_custom_call" | custom-call | bytes 6000000 | tf_op jit(solution)/shard_map/last/pallas_call | solution.py:592
  52.7 22.3 %all_to_all.5.parts = f32[8,3,8,768]{3,2,1,0:T(8,128)S(1)} all-to-all(f32[8,3,8,768]{3,2,1,0:T(8,128)S(1)} %get-tuple-element.105), channel_id=1, replica_groups=mesh['dom'=4,'event'=8] {'event'}, dimensions={0} | all-to-all | bytes 1179648 | tf_op jit(solution)/shard_map/all_to_all | solution.py:709
  75.0 0.7 event_sum.1
Async XLA Ops:
  0.6 7.7 %copy-start.5 = (bf16[192,192]{1,0:T(8,128)(2,1)S(1)}, bf16[192,192]{1,0:T(8,128)(2,1)}, u32[]{:S(2)}) copy-start(bf16[192,192]{1,0:T(8,128)(2,1)} %constant.25.clone.vel) | copy-start | bytes 221188
  0.6 7.6 %copy-start.2 = (f32[64,768]{1,0:T(8,128)S(1)}, f32[64,768]{1,0:T(8,128)}, u32[]{:S(2)}) copy-start(f32[64,768]{1,0:T(8,128)} %shear.11) | copy-start | bytes 589828
  0.7 7.6 %copy-start.1 = (f32[64,768]{1,0:T(8,128)S(1)}, f32[64,768]{1,0:T(8,128)}, u32[]{:S(2)}) copy-start(f32[64,768]{1,0:T(8,128)} %lame.11) | copy-start | bytes 589828
  3.2 6.9 %collective-permute-start = (f32[168,128]{1,0:T(8,128)S(1)}, f32[168,128]{1,0:T(8,128)S(1)}, u32[]{:S(2)}, u32[]{:S(2)}) collective-permute-start(f32[168,128]{1,0:T(8,128)S(1)} %get-tuple-element.60), channel_id=1, source_target_pairs={{8,16},{16,8},{9,17},{17,9},{10,18},{18,10},{11,19},{19,11},{12,20... | collective-permute-start | bytes 258056 | tf_op jit(solution)/shard_map/ppermute | solution.py:611
  3.9 6.2 %collective-permute-start.1 = (f32[168,128]{1,0:T(8,128)S(1)}, f32[168,128]{1,0:T(8,128)S(1)}, u32[]{:S(2)}, u32[]{:S(2)}) collective-permute-start(f32[168,128]{1,0:T(8,128)S(1)} %get-tuple-element.61), channel_id=1, source_target_pairs={{0,8},{8,0},{16,24},{24,16},{1,9},{9,1},{17,25},{25,17},{2,10},{10... | collective-permute-start | bytes 258056 | tf_op jit(solution)/shard_map/ppermute | solution.py:611
  10.1 6.3 %copy-start = (f32[1,3,3,64,768]{4,3,2,1,0:T(8,128)S(1)}, f32[1,3,3,64,768]{4,3,2,1,0:T(8,128)}, u32[]{:S(2)}) copy-start(f32[1,3,3,64,768]{4,3,2,1,0:T(8,128)} %param.11) | copy-start | bytes 5308420
  10.1 6.3 %copy-start.3 = (f32[64,768]{1,0:T(8,128)S(1)}, f32[64,768]{1,0:T(8,128)}, u32[]{:S(2)}) copy-start(f32[64,768]{1,0:T(8,128)} %density.5) | copy-start | bytes 589828
  10.1 6.3 %copy-start.4 = (bf16[192,192]{1,0:T(8,128)(2,1)S(1)}, bf16[192,192]{1,0:T(8,128)(2,1)}, u32[]{:S(2)}) copy-start(bf16[192,192]{1,0:T(8,128)(2,1)} %constant.26.clone.fwd) | copy-start | bytes 221188
  10.1 6.3 %copy-start.6 = (bf16[64,576]{1,0:T(8,128)(2,1)S(1)}, bf16[64,576]{1,0:T(8,128)(2,1)}, u32[]{:S(2)}) copy-start(bf16[64,576]{1,0:T(8,128)(2,1)} %constant.27.clone.div) | copy-start | bytes 221188
  12.5 5.9 %collective-permute-start.2 = (f32[168,128]{1,0:T(8,128)S(1)}, f32[168,128]{1,0:T(8,128)S(1)}, u32[]{:S(2)}, u32[]{:S(2)}) collective-permute-start(f32[168,128]{1,0:T(8,128)S(1)} %get-tuple-element.72), channel_id=1, source_target_pairs={{8,16},{16,8},{9,17},{17,9},{10,18},{18,10},{11,19},{19,11},{12,20... | collective-permute-start | bytes 258056 | tf_op jit(solution)/shard_map/ppermute | solution.py:611
  13.1 5.3 %collective-permute-start.3 = (f32[168,128]{1,0:T(8,128)S(1)}, f32[168,128]{1,0:T(8,128)S(1)}, u32[]{:S(2)}, u32[]{:S(2)}) collective-permute-start(f32[168,128]{1,0:T(8,128)S(1)} %get-tuple-element.73), channel_id=1, source_target_pairs={{0,8},{8,0},{16,24},{24,16},{1,9},{9,1},{17,25},{25,17},{2,10},{10... | collective-permute-start | bytes 258056 | tf_op jit(solution)/shard_map/ppermute | solution.py:611
  20.6 5.7 %collective-permute-start.4 = (f32[168,128]{1,0:T(8,128)S(1)}, f32[168,128]{1,0:T(8,128)S(1)}, u32[]{:S(2)}, u32[]{:S(2)}) collective-permute-start(f32[168,128]{1,0:T(8,128)S(1)} %get-tuple-element.79), channel_id=1, source_target_pairs={{8,16},{16,8},{9,17},{17,9},{10,18},{18,10},{11,19},{19,11},{12,20... | collective-permute-start | bytes 258056 | tf_op jit(solution)/shard_map/ppermute | solution.py:611
  21.4 4.8 %collective-permute-start.5 = (f32[168,128]{1,0:T(8,128)S(1)}, f32[168,128]{1,0:T(8,128)S(1)}, u32[]{:S(2)}, u32[]{:S(2)}) collective-permute-start(f32[168,128]{1,0:T(8,128)S(1)} %get-tuple-element.80), channel_id=1, source_target_pairs={{0,8},{8,0},{16,24},{24,16},{1,9},{9,1},{17,25},{25,17},{2,10},{10... | collective-permute-start | bytes 258056 | tf_op jit(solution)/shard_map/ppermute | solution.py:611
  28.6 5.9 %collective-permute-start.6 = (f32[168,128]{1,0:T(8,128)S(1)}, f32[168,128]{1,0:T(8,128)S(1)}, u32[]{:S(2)}, u32[]{:S(2)}) collective-permute-start(f32[168,128]{1,0:T(8,128)S(1)} %get-tuple-element.86), channel_id=1, source_target_pairs={{8,16},{16,8},{9,17},{17,9},{10,18},{18,10},{11,19},{19,11},{12,20... | collective-permute-start | bytes 258056 | tf_op jit(solution)/shard_map/ppermute | solution.py:611
  29.2 5.2 %collective-permute-start.7 = (f32[168,128]{1,0:T(8,128)S(1)}, f32[168,128]{1,0:T(8,128)S(1)}, u32[]{:S(2)}, u32[]{:S(2)}) collective-permute-start(f32[168,128]{1,0:T(8,128)S(1)} %get-tuple-element.87), channel_id=1, source_target_pairs={{0,8},{8,0},{16,24},{24,16},{1,9},{9,1},{17,25},{25,17},{2,10},{10... | collective-permute-start | bytes 258056 | tf_op jit(solution)/shard_map/ppermute | solution.py:611
  36.6 5.5 %collective-permute-start.8 = (f32[168,128]{1,0:T(8,128)S(1)}, f32[168,128]{1,0:T(8,128)S(1)}, u32[]{:S(2)}, u32[]{:S(2)}) collective-permute-start(f32[168,128]{1,0:T(8,128)S(1)} %get-tuple-element.93), channel_id=1, source_target_pairs={{8,16},{16,8},{9,17},{17,9},{10,18},{18,10},{11,19},{19,11},{12,20... | collective-permute-start | bytes 258056 | tf_op jit(solution)/shard_map/ppermute | solution.py:611
  37.3 4.9 %collective-permute-start.9 = (f32[168,128]{1,0:T(8,128)S(1)}, f32[168,128]{1,0:T(8,128)S(1)}, u32[]{:S(2)}, u32[]{:S(2)}) collective-permute-start(f32[168,128]{1,0:T(8,128)S(1)} %get-tuple-element.94), channel_id=1, source_target_pairs={{0,8},{8,0},{16,24},{24,16},{1,9},{9,1},{17,25},{25,17},{2,10},{10... | collective-permute-start | bytes 258056 | tf_op jit(solution)/shard_map/ppermute | solution.py:611
  44.5 6.2 %collective-permute-start.10 = (f32[168,128]{1,0:T(8,128)S(1)}, f32[168,128]{1,0:T(8,128)S(1)}, u32[]{:S(2)}, u32[]{:S(2)}) collective-permute-start(f32[168,128]{1,0:T(8,128)S(1)} %get-tuple-element.100), channel_id=1, source_target_pairs={{8,16},{16,8},{9,17},{17,9},{10,18},{18,10},{11,19},{19,11},{12,20... | collective-permute-start | bytes 258056 | tf_op jit(solution)/shard_map/ppermute | solution.py:611
  45.4 5.4 %collective-permute-start.11 = (f32[168,128]{1,0:T(8,128)S(1)}, f32[168,128]{1,0:T(8,128)S(1)}, u32[]{:S(2)}, u32[]{:S(2)}) collective-permute-start(f32[168,128]{1,0:T(8,128)S(1)} %get-tuple-element.101), channel_id=1, source_target_pairs={{0,8},{8,0},{16,24},{24,16},{1,9},{9,1},{17,25},{25,17},{2,10},{10... | collective-permute-start | bytes 258056 | tf_op jit(solution)/shard_map/ppermute | solution.py:611

commit v3 on v1

--- a/solution.py
+++ b/solution.py
@@ -17,6 +17,7 @@
 CHUNK = 256
 MAIN = 384
 TAIL = 64
+HALO = 512
 SEND_MAIN = 48 * MAIN // 128
 SEND_ROWS = SEND_MAIN + 48 * TAIL // 128
 VMEM_LIMIT = 40 * 2**20
@@ -184,18 +185,15 @@
     )
 
 
-def halo_faces(lhs, tail, keys, hots, lanes, width):
-    blocks = 2 * MAIN // CHUNK
-    first = width // CHUNK
+def halo_faces(lhs, keys, hots, lanes, width):
+    blocks = HALO // CHUNK
+    first = width // CHUNK + blocks
     out = []
     for f in range(6):
         key = keys[f:f + 1]
         got = mm(lhs, hots[f, :, lanes])
         which = key >> 8
-        late = jnp.concatenate(
-            [gather_tile(tail, key[:, t:t + 128] & 127) for t in range(0, CHUNK, 128)], axis=1
-        )
-        total = jnp.where(which == first + blocks, late, 0.0)
+        total = jnp.zeros((48, CHUNK), f32)
         for a in range(blocks):
             both = got[48 * a:48 * a + 48] + got[48 * (blocks + a):48 * (blocks + a) + 48]
             total = jnp.where(which == first + a, both, total)
@@ -203,24 +201,17 @@
     return out
 
 
-def halo_lhs(recv_one, recv_two):
-    tiles = [
-        recv[48 * t:48 * t + 48] for recv in (recv_one, recv_two) for t in range(MAIN // 128)
-    ]
+def halo_lhs(recv):
+    late = recv[SEND_MAIN:SEND_ROWS]
+    late = jnp.concatenate([late[:, 0:TAIL], late[:, TAIL:2 * TAIL]], axis=0)
+    late = jnp.concatenate([late, jnp.zeros((48, 128 - TAIL), f32)], axis=1)
+    tiles = [recv[48 * t:48 * t + 48] for t in range(MAIN // 128)] + [late]
     blocks = [jnp.concatenate(tiles[t:t + 2], axis=1) for t in range(0, len(tiles), 2)]
     high, low = split(jnp.concatenate(blocks, axis=0))
-    one, two = recv_one[SEND_MAIN:SEND_ROWS], recv_two[SEND_MAIN:SEND_ROWS]
-    tail = jnp.concatenate(
-        [
-            jnp.concatenate([one[:, 0:TAIL], two[:, 0:TAIL]], axis=1),
-            jnp.concatenate([one[:, TAIL:2 * TAIL], two[:, TAIL:2 * TAIL]], axis=1),
-        ],
-        axis=0,
-    )
-    return jnp.concatenate([high, low], axis=0), tail
-
-
-def local_faces(traces, keys, hots, lanes, own_sign):
+    return jnp.concatenate([high, low], axis=0)
+
+
+def local_faces(traces, near, keys, hots, lanes, own_sign):
     width = traces.shape[1]
     blocks = width // CHUNK
     out = []
@@ -228,7 +219,9 @@
         key = keys[f:f + 1]
         other = 48 * (f ^ 1)
         lhs = jnp.concatenate(
-            [traces[p + other:p + other + 48, s] for p in (0, 288) for s in chunks(width)], axis=0
+            [traces[p + other:p + other + 48, s] for p in (0, 288) for s in chunks(width)]
+            + [near],
+            axis=0,
         )
         got = mm(lhs, hots[f, :, lanes])
         which = key >> 8
@@ -238,6 +231,11 @@
         for a in range(blocks):
             both = got[48 * a:48 * a + 48] + got[48 * (blocks + a):48 * (blocks + a) + 48]
             total = jnp.where(which == a, both, total)
+        for a in range(HALO // CHUNK):
+            at = 96 * blocks + 48 * a
+            low = at + 48 * (HALO // CHUNK)
+            both = got[at:at + 48] + got[low:low + 48]
+            total = jnp.where(which == blocks + a, both, total)
         out.append(total)
     return out
 
@@ -322,7 +320,7 @@
 
 
 def start_kernel(
-    even, state_hbm, neighbour_hbm, send_list_hbm,
+    down, state_hbm, neighbour_hbm, send_list_hbm,
     velocity, stress, keys, picks, faces, late, traces, send_one, send_two,
     state, neighbour, send_list, values, stage, sems,
 ):
@@ -339,14 +337,12 @@
         copy.wait()
     width = neighbour.shape[1]
     cap = send_list.shape[1]
-    is_even = even[0] == 1
+    is_down = down[0] == 1
     code = neighbour[...]
     low = code < width + cap
     at = code - width - jnp.where(low, 0, cap)
-    second = jnp.where(low == is_even, 0, 1)
-    place = jnp.where(
-        at < MAIN, at + MAIN * second, at - MAIN + 2 * MAIN + TAIL * second
-    )
+    second = jnp.where(low == is_down, 0, 1)
+    place = at + HALO * second
     keys[...] = jnp.where(code < width, code, width + place)
     valid = jnp.where(jnp.max(code, axis=0, keepdims=True) >= 0, 1.0, 0.0)
     entries = send_list[...]
@@ -354,7 +350,7 @@
         [entries, jnp.full((2, MAIN + TAIL - cap), -1, jnp.int32)], axis=1
     )
     one, two = entries[0:1], entries[1:2]
-    one, two = jnp.where(is_even, one, two), jnp.where(is_even, two, one)
+    one, two = jnp.where(is_down, one, two), jnp.where(is_down, two, one)
     late[...] = jnp.concatenate([one[:, MAIN:], two[:, MAIN:]], axis=1)
     main = jnp.concatenate([one[:, 0:MAIN], two[:, 0:MAIN]], axis=1)
     face = jnp.zeros_like(main)
@@ -379,11 +375,12 @@
 
 
 def vel_local_kernel(
-    step, velocity, stress, traces, keys, lame, shear, vel, *rest,
+    step, velocity, stress, traces, recv, keys, lame, shear, vel, *rest,
 ):
     total = None
     *rest, scratch = rest
     scratch[...] = jnp.zeros(scratch.shape, f32)
+    near = halo_lhs(recv)
     if step < 0:
         stress_out, jump_out, hots, lame_scaled, shear_scaled = rest
     elif step == 0:
@@ -397,7 +394,7 @@
                 hots[f, :, lanes] = onehot(keys[f:f + 1, lanes] & (CHUNK - 1), CHUNK)
             lame_scaled[:, lanes] = (lift_half * time_step) * lame[:, lanes]
             shear_scaled[:, lanes] = (lift_half * time_step) * shear[:, lanes]
-        plus = local_faces(traces, keys[:, lanes], hots, lanes, 1.0)
+        plus = local_faces(traces, near, keys[:, lanes], hots, lanes, 1.0)
         grad, jump = lift_velocity(plus, scratch, lanes)
         count = holders(CHUNK)
         whole = []
@@ -423,14 +420,14 @@
 
 
 def vel_halo_kernel(
-    stress, jump, recv_one, recv_two, keys, hots, picks, faces, late, lame_scaled, shear_scaled,
+    stress, jump, recv, keys, hots, picks, faces, late, lame_scaled, shear_scaled,
     stress_out, jump_out, traces, send_one, send_two, values, scratch, stage,
 ):
     width = stress.shape[2]
     scratch[...] = jnp.zeros(scratch.shape, f32)
-    lhs, tail = halo_lhs(recv_one, recv_two)
+    lhs = halo_lhs(recv)
     for lanes in chunks(width):
-        plus = halo_faces(lhs, tail, keys[:, lanes], hots, lanes, width)
+        plus = halo_faces(lhs, keys[:, lanes], hots, lanes, width)
         grad, more = lift_velocity(plus, scratch, lanes)
         rate = rate_of(grad, lame_scaled[:, lanes], shear_scaled[:, lanes])
         now = [stress[m, :, lanes] + rate[m] for m in range(6)]
@@ -443,10 +440,11 @@
 
 
 def str_local_kernel(
-    step, velocity, stress, jump, traces, keys, hots, density, lame, shear, forward, div, fwd, *rest,
+    step, velocity, stress, jump, traces, recv, keys, hots, density, lame, shear, forward, div, fwd, *rest,
 ):
     *rest, scratch = rest
     scratch[...] = jnp.zeros(scratch.shape, f32)
+    near = halo_lhs(recv)
     if step == 0:
         total = None
         velocity_out, total_out, scale_out = rest
@@ -454,7 +452,7 @@
         total, velocity_out, total_out = rest
     width = velocity.shape[2]
     for lanes in chunks(width):
-        plus = local_faces(traces, keys[:, lanes], hots, lanes, -1.0)
+        plus = local_faces(traces, near, keys[:, lanes], hots, lanes, -1.0)
         lifted = lift_stress(plus, scratch, lanes)
         now = [stress[m, :, lanes] for m in range(6)]
         pieces = [split(s) for s in now]
@@ -496,17 +494,17 @@
 
 
 def str_halo_kernel(
-    velocity, recv_one, recv_two, keys, hots, picks, faces, late, scale,
+    velocity, recv, keys, hots, picks, faces, late, scale,
     velocity_out, traces, send_one, send_two, values, scratch, stage,
 ):
     halo_velocity(
-        velocity, recv_one, recv_two, keys, hots, scale, velocity_out, traces, values, scratch, stage
+        velocity, recv, keys, hots, scale, velocity_out, traces, values, scratch, stage
     )
     pack(traces, values, picks, faces, late, send_one, send_two)
 
 
 def last_kernel(
-    step, velocity, recv_one, recv_two, keys, hots, scale, forward, other, *rest
+    step, velocity, recv, keys, hots, scale, forward, other, *rest
 ):
     *total, velocity_out, total_out, scratch, buffer, sems = rest
     total = total[0] if total else None
@@ -528,7 +526,7 @@
                 total_out[e, m + 1, :, lanes] = other[e, m, :, lanes]
 
     halo_velocity(
-        velocity, recv_one, recv_two, keys, hots, scale, buffer, None, None, scratch, None, finish
+        velocity, recv, keys, hots, scale, buffer, None, None, scratch, None, finish
     )
     for copy in copies:
         copy.wait()
@@ -545,14 +543,14 @@
 
 
 def halo_velocity(
-    velocity, recv_one, recv_two, keys, hots, scale, velocity_out, traces, values, scratch, stage,
+    velocity, recv, keys, hots, scale, velocity_out, traces, values, scratch, stage,
     finish=None,
 ):
     width = velocity.shape[2]
     scratch[...] = jnp.zeros(scratch.shape, f32)
-    lhs, tail = halo_lhs(recv_one, recv_two)
+    lhs = halo_lhs(recv)
     for lanes in chunks(width):
-        plus = halo_faces(lhs, tail, keys[:, lanes], hots, lanes, width)
+        plus = halo_faces(lhs, keys[:, lanes], hots, lanes, width)
         lifted = lift_stress(plus, scratch, lanes)
         now = [velocity[i, :, lanes] + scale[:, lanes] * lifted[i] for i in range(3)]
         for i in range(3):
@@ -583,7 +581,7 @@
     got = []
     for first, value in enumerate(sent):
         pairs = []
-        for low in range(1 - first, count - 1, 2):
+        for low in range(first, count - 1, 2):
             pairs += [(low, low + 1), (low + 1, low)]
         got.append(lax.ppermute(value, axis, pairs))
     return got
@@ -597,7 +595,7 @@
     table = {k: jnp.asarray(v) for k, v in tables().items()}
     state = adjoint_state[0]
     forward = forward_velocity[0]
-    even = (1 - lax.axis_index("dom") % 2).astype(jnp.int32).reshape(1)
+    down = (lax.axis_index("dom") % 2).astype(jnp.int32).reshape(1)
 
     nodal = pltpu.VMEM((3, width // 128, 64, 128), f32)
     values = pltpu.VMEM((288, width), f32)
@@ -616,7 +614,7 @@
 
     velocity, stress, keys, picks, faces, late, traces, *sent = call(
         "start", start_kernel,
-        (even, *(pltpu.with_memory_space_constraint(x, pltpu.HBM)
+        (down, *(pltpu.with_memory_space_constraint(x, pltpu.HBM)
                 for x in (state, neighbour, send_list))),
         [vector, tensor] + lists + [trace] + sends,
         specs={0: pl.BlockSpec(memory_space=pltpu.SMEM)}
@@ -628,8 +626,8 @@
     )
     rho_total = other_total = hots = None
     for n in range(steps):
-        recv = swap(sent, "dom")
-        args = [velocity, stress, traces, keys, lame_lambda, shear_modulus,
+        first, recv = swap(sent, "dom")
+        args = [velocity, stress, traces, first, keys, lame_lambda, shear_modulus,
                 table["vel"]]
         outs = [tensor, vector]
         if n:
@@ -647,11 +645,11 @@
             hots, lame_scaled, shear_scaled = more
         stress, jump, traces, *sent = call(
             "vel_halo", vel_halo_kernel,
-            (stress, jump, *recv, keys, hots, picks, faces, late, lame_scaled, shear_scaled),
+            (stress, jump, recv, keys, hots, picks, faces, late, lame_scaled, shear_scaled),
             [tensor, vector, trace] + sends, scratch=[values, nodal, nodal],
         )
-        recv = swap(sent, "dom")
-        args = [velocity, stress, jump, traces, keys, hots, density, lame_lambda, shear_modulus,
+        first, recv = swap(sent, "dom")
+        args = [velocity, stress, jump, traces, first, keys, hots, density, lame_lambda, shear_modulus,
                 forward, table["div"], table["fwd"]]
         if n:
             args += [other_total]
@@ -664,13 +662,13 @@
         if n < steps - 1:
             velocity, traces, *sent = call(
                 "str_halo", str_halo_kernel,
-                (velocity, *recv, keys, hots, picks, faces, late, scale),
+                (velocity, recv, keys, hots, picks, faces, late, scale),
                 [vector, trace] + sends, scratch=[values, nodal, nodal],
             )
         else:
             velocity, kernel_total = call(
                 "last", functools.partial(last_kernel, n),
-                (velocity, *recv, keys, hots, scale, forward, other_total)
+                (velocity, recv, keys, hots, scale, forward, other_total)
                 + ((rho_total,) if n else ()),
                 [vector, three],
                 scratch=[

time: 75.3 us -> 71.9 us (0.955)
  starting transfers between devices: 24.9 us -> 19.5 us
  waiting for transfers between devices: 0.03 us -> 1.43 us
    ppermute x12, starting transfers between devices: 24.9 us -> 19.5 us  [swap(): got.append(lax.ppermute(value, axis, pairs))]
    ppermute x12, waiting for transfers between devices: 0.03 us -> 1.43 us  [swap(): got.append(lax.ppermute(value, axis, pairs))]
  transfers between devices with their start and end apart: 12 -> 12, of which waited for: 0 -> 6; matrix products, arithmetic and copies ran while one was open for 0% -> 0% of each run, Pallas kernels for 14% -> 19%
where the time goes in v3:
time: 71.9 us; the launch traced here: 70.9 us
  Pallas kernels  26.6 us (37%)
  blocking collectives  22.4 us (31%)
  starting transfers between devices  19.5 us (27%)
  waiting for transfers between devices  1.43 us (2%)
  between operations  0.89 us (1%)
    pallas_call x14, Pallas kernels, call(): pl.pallas_call(kernel, name=name, in_specs=[specs.get(k, whole) for k in...  26.6 us
    all_to_all x1, blocking collectives, local(): parts = lax.all_to_all(kernel_total, 'event', 0, 0, tiled=True)  22.4 us
    ppermute x12, starting transfers between devices, swap(): got.append(lax.ppermute(value, axis, pairs))  19.5 us
  transfers between devices with their start and end apart: 12, of which 6 were waited for; matrix products, arithmetic and copies ran while one was open for 0% of the time, Pallas kernels for 19%

profile of v3, /device:TPU:0, one launch (start us, length us, event | category | flops | bytes accessed | tf_op | source)
XLA Modules:
  0.0 70.9 jit_solution(846915163469075956)
XLA Ops:
  0.6 0.0 copy-start.5
  0.6 0.0 copy-start.2
  0.7 0.0 copy-start.1
  0.7 2.4 %start.1 = (f32[3,64,768]{2,1,0:T(8,128)S(1)}, f32[6,64,768]{2,1,0:T(8,128)S(1)}, s32[6,768]{1,0:T(8,128)S(1)}, bf16[768,768]{1,0:T(8,128)(2,1)S(1)}, s32[1,768]...) custom-call(s32[1]{0:T(128)} %bitcast.down, ...), custom_call_target="tpu_custom_call" | custom-call | bytes 6000000 | tf_op jit(solution)/shard_map/start/pallas_call | solution.py:567
  3.1 0.5 collective-permute-start
  3.6 0.7 collective-permute-start.1
  4.3 0.3 collective-permute-done.recv
  4.6 0.0 copy-done.5
  4.6 0.0 copy-done.2
  4.6 0.0 copy-done.1
  4.6 2.2 %vel_local.3 = (f32[6,64,768]{2,1,0:T(8,128)S(1)}, f32[3,64,768]{2,1,0:T(8,128)S(1)}, bf16[6,256,768]{2,1,0:T(8,128)(2,1)S(1)}, f32[64,768]{1,0:T(8,128)S(1)}, f32[64,768]{1,0:T(8,128)S(1)}) custom-call(f32[3,64,768]{2,1,0:T(8,128)S(1)} %get-tuple-element.54.velocity, f32[6,64,768]{2,1,0:T(8,128)S(1)} %get-tuple-element.55.stress, ...), custom_call_target="tpu_custom_call" | custom-call | flops 4000000000 | bytes 6000000 | tf_op jit(solution)/shard_map/vel_local/pallas_call | solution.py:567
  6.7 0.0 collective-permute-done.1.recv
  6.7 0.0 copy-start
  6.8 0.0 copy-start.3
  6.8 0.0 copy-start.4
  6.8 0.0 copy-start.6
  6.8 1.8 %vel_halo.3 = (f32[6,64,768]{2,1,0:T(8,128)S(1)}, f32[3,64,768]{2,1,0:T(8,128)S(1)}, bf16[576,768]{1,0:T(8,128)(2,1)S(1)}, f32[168,128]{1,0:T(8,128)S(1)}, f32[168,128]{1,0:T(8,128)S(1)}) custom-call(f32[6,64,768]{2,1,0:T(8,128)S(1)} %get-tuple-element.59.stress, f32[3,64,768]{2,1,0:T(8,128)S(1)} %get-tuple-element.60.jump, ...), custom_call_target="tpu_custom_call" | custom-call | bytes 6000000 | tf_op jit(solution)/shard_map/vel_halo/pallas_call | solution.py:567
  8.6 3.7 %collective-permute-start.2 = (f32[168,128]{1,0:T(8,128)S(1)}, f32[168,128]{1,0:T(8,128)S(1)}, u32[]{:S(2)}, u32[]{:S(2)}) collective-permute-start(f32[168,128]{1,0:T(8,128)S(1)} %get-tuple-element.71), channel_id=1, source_target_pairs={{0,8},{8,0},{16,24},{24,16},{1,9},{9,1},{17,25},{25,17},{2,10},{10... | collective-permute-start | bytes 258056 | tf_op jit(solution)/shard_map/ppermute | solution.py:586
  12.3 0.7 collective-permute-start.3
  13.0 0.3 collective-permute-done.2.recv
  13.2 0.0 copy-done
  13.2 0.0 copy-done.3
  13.2 0.0 copy-done.4
  13.2 0.0 copy-done.6
  13.2 2.4 %str_local.3 = (f32[3,64,768]{2,1,0:T(8,128)S(1)}, f32[8,2,8,768]{3,2,1,0:T(8,128)S(1)}, f32[64,768]{1,0:T(8,128)S(1)}) custom-call(f32[3,64,768]{2,1,0:T(8,128)S(1)} %get-tuple-element.54.velocity, f32[6,64,768]{2,1,0:T(8,128)S(1)} %get-tuple-element.68.stress, f32[3,64,768]{2,1,0:T(8,128)S(1)} %get-tuple-element.69.jump, ...), custom_call_target="tpu_custom_call" | custom-call | flops 4000000000 | bytes 6000000 | tf_op jit(solution)/shard_map/str_local/pallas_call | solution.py:567
  15.6 0.0 collective-permute-done.3.recv
  15.6 1.6 %str_halo.2 = (f32[3,64,768]{2,1,0:T(8,128)S(1)}, bf16[576,768]{1,0:T(8,128)(2,1)S(1)}, f32[168,128]{1,0:T(8,128)S(1)}, f32[168,128]{1,0:T(8,128)S(1)}) custom-call(f32[3,64,768]{2,1,0:T(8,128)S(1)} %get-tuple-element.72.velocity, f32[168,128]{1,0:T(8,128)S(1)} %collective-permute-done.3.recv, s32[6,768]{1,0:T(8,128)S(1)} %get-tuple-element.58.keys, ...), custom_call_target="tpu_custom_call" | custom-call | bytes 6000000 | tf_op jit(solution)/shard_map/str_halo/pallas_call | solution.py:567
  17.3 2.7 %collective-permute-start.4 = (f32[168,128]{1,0:T(8,128)S(1)}, f32[168,128]{1,0:T(8,128)S(1)}, u32[]{:S(2)}, u32[]{:S(2)}) collective-permute-start(f32[168,128]{1,0:T(8,128)S(1)} %get-tuple-element.77), channel_id=1, source_target_pairs={{0,8},{8,0},{16,24},{24,16},{1,9},{9,1},{17,25},{25,17},{2,10},{10... | collective-permute-start | bytes 258056 | tf_op jit(solution)/shard_map/ppermute | solution.py:586
  20.0 0.7 collective-permute-start.5
  20.6 0.3 collective-permute-done.4.recv
  20.9 2.0 %vel_local.4 = (f32[6,64,768]{2,1,0:T(8,128)S(1)}, f32[3,64,768]{2,1,0:T(8,128)S(1)}, f32[64,768]{1,0:T(8,128)S(1)}) custom-call(f32[3,64,768]{2,1,0:T(8,128)S(1)} %get-tuple-element.75.velocity, f32[6,64,768]{2,1,0:T(8,128)S(1)} %get-tuple-element.68.stress, bf16[576,768]{1,0:T(8,128)(2,1)S(1)} %get-tuple-element.76.traces, ...), custom_call_target="tpu_custom_call" | custom-call | flops 4000000000 | bytes 6000000 | tf_op jit(solution)/shard_map/vel_local/pallas_call | solution.py:567
  23.0 0.0 collective-permute-done.5.recv
  23.0 1.8 %vel_halo.4 = (f32[6,64,768]{2,1,0:T(8,128)S(1)}, f32[3,64,768]{2,1,0:T(8,128)S(1)}, bf16[576,768]{1,0:T(8,128)(2,1)S(1)}, f32[168,128]{1,0:T(8,128)S(1)}, f32[168,128]{1,0:T(8,128)S(1)}) custom-call(f32[6,64,768]{2,1,0:T(8,128)S(1)} %get-tuple-element.78.stress, f32[3,64,768]{2,1,0:T(8,128)S(1)} %get-tuple-element.79.jump, ...), custom_call_target="tpu_custom_call" | custom-call | bytes 6000000 | tf_op jit(solution)/shard_map/vel_halo/pallas_call | solution.py:567
  24.7 2.9 %collective-permute-start.6 = (f32[168,128]{1,0:T(8,128)S(1)}, f32[168,128]{1,0:T(8,128)S(1)}, u32[]{:S(2)}, u32[]{:S(2)}) collective-permute-start(f32[168,128]{1,0:T(8,128)S(1)} %get-tuple-element.84), channel_id=1, source_target_pairs={{0,8},{8,0},{16,24},{24,16},{1,9},{9,1},{17,25},{25,17},{2,10},{10... | collective-permute-start | bytes 258056 | tf_op jit(solution)/shard_map/ppermute | solution.py:586
  27.6 0.8 %collective-permute-start.7 = (f32[168,128]{1,0:T(8,128)S(1)}, f32[168,128]{1,0:T(8,128)S(1)}, u32[]{:S(2)}, u32[]{:S(2)}) collective-permute-start(f32[168,128]{1,0:T(8,128)S(1)} %get-tuple-element.87), channel_id=1, source_target_pairs={{8,16},{16,8},{9,17},{17,9},{10,18},{18,10},{11,19},{19,11},{12,20... | collective-permute-start | bytes 258056 | tf_op jit(solution)/shard_map/ppermute | solution.py:586
  28.5 0.1 collective-permute-done.6.recv
  28.6 2.4 %str_local.4 = (f32[3,64,768]{2,1,0:T(8,128)S(1)}, f32[8,2,8,768]{3,2,1,0:T(8,128)S(1)}) custom-call(f32[3,64,768]{2,1,0:T(8,128)S(1)} %get-tuple-element.75.velocity, f32[6,64,768]{2,1,0:T(8,128)S(1)} %get-tuple-element.81.stress, f32[3,64,768]{2,1,0:T(8,128)S(1)} %get-tuple-element.82.jump, bf16[576,768]{1,0:T(8,128)(2,1)S(1)} %get-tuple-element.83.traces, ...), custom_call_target="tpu_custom_call" | custom-call | flops 4000000000 | bytes 6000000 | tf_op jit(solution)/shard_map/str_local/pallas_call | solution.py:567
  31.0 0.0 collective-permute-done.7.recv
  31.0 1.6 %str_halo.3 = (f32[3,64,768]{2,1,0:T(8,128)S(1)}, bf16[576,768]{1,0:T(8,128)(2,1)S(1)}, f32[168,128]{1,0:T(8,128)S(1)}, f32[168,128]{1,0:T(8,128)S(1)}) custom-call(f32[3,64,768]{2,1,0:T(8,128)S(1)} %get-tuple-element.86.velocity, f32[168,128]{1,0:T(8,128)S(1)} %collective-permute-done.7.recv, s32[6,768]{1,0:T(8,128)S(1)} %get-tuple-element.58.keys, ...), custom_call_target="tpu_custom_call" | custom-call | bytes 6000000 | tf_op jit(solution)/shard_map/str_halo/pallas_call | solution.py:567
  32.6 2.7 %collective-permute-start.8 = (f32[168,128]{1,0:T(8,128)S(1)}, f32[168,128]{1,0:T(8,128)S(1)}, u32[]{:S(2)}, u32[]{:S(2)}) collective-permute-start(f32[168,128]{1,0:T(8,128)S(1)} %get-tuple-element.90), channel_id=1, source_target_pairs={{0,8},{8,0},{16,24},{24,16},{1,9},{9,1},{17,25},{25,17},{2,10},{10... | collective-permute-start | bytes 258056 | tf_op jit(solution)/shard_map/ppermute | solution.py:586
  35.3 0.7 collective-permute-start.9
  36.0 0.3 collective-permute-done.8.recv
  36.2 2.1 %vel_local.5 = (f32[6,64,768]{2,1,0:T(8,128)S(1)}, f32[3,64,768]{2,1,0:T(8,128)S(1)}, f32[64,768]{1,0:T(8,128)S(1)}) custom-call(f32[3,64,768]{2,1,0:T(8,128)S(1)} %get-tuple-element.88.velocity, f32[6,64,768]{2,1,0:T(8,128)S(1)} %get-tuple-element.81.stress, bf16[576,768]{1,0:T(8,128)(2,1)S(1)} %get-tuple-element.89.traces, ...), custom_call_target="tpu_custom_call" | custom-call | flops 4000000000 | bytes 6000000 | tf_op jit(solution)/shard_map/vel_local/pallas_call | solution.py:567
  38.3 0.0 collective-permute-done.9.recv
  38.3 1.8 %vel_halo.5 = (f32[6,64,768]{2,1,0:T(8,128)S(1)}, f32[3,64,768]{2,1,0:T(8,128)S(1)}, bf16[576,768]{1,0:T(8,128)(2,1)S(1)}, f32[168,128]{1,0:T(8,128)S(1)}, f32[168,128]{1,0:T(8,128)S(1)}) custom-call(f32[6,64,768]{2,1,0:T(8,128)S(1)} %get-tuple-element.92.stress, f32[3,64,768]{2,1,0:T(8,128)S(1)} %get-tuple-element.93.jump, ...), custom_call_target="tpu_custom_call" | custom-call | bytes 6000000 | tf_op jit(solution)/shard_map/vel_halo/pallas_call | solution.py:567
  40.1 2.9 %collective-permute-start.10 = (f32[168,128]{1,0:T(8,128)S(1)}, f32[168,128]{1,0:T(8,128)S(1)}, u32[]{:S(2)}, u32[]{:S(2)}) collective-permute-start(f32[168,128]{1,0:T(8,128)S(1)} %get-tuple-element.98), channel_id=1, source_target_pairs={{0,8},{8,0},{16,24},{24,16},{1,9},{9,1},{17,25},{25,17},{2,10},{10... | collective-permute-start | bytes 258056 | tf_op jit(solution)/shard_map/ppermute | solution.py:586
  43.0 0.7 collective-permute-start.11
  43.6 0.3 collective-permute-done.10.recv
  43.9 2.4 %str_local.5 = (f32[3,64,768]{2,1,0:T(8,128)S(1)}, f32[8,2,8,768]{3,2,1,0:T(8,128)S(1)}) custom-call(f32[3,64,768]{2,1,0:T(8,128)S(1)} %get-tuple-element.88.velocity, f32[6,64,768]{2,1,0:T(8,128)S(1)} %get-tuple-element.95.stress, f32[3,64,768]{2,1,0:T(8,128)S(1)} %get-tuple-element.96.jump, bf16[576,768]{1,0:T(8,128)(2,1)S(1)} %get-tuple-element.97.traces, ...), custom_call_target="tpu_custom_call" | custom-call | flops 4000000000 | bytes 6000000 | tf_op jit(solution)/shard_map/str_local/pallas_call | solution.py:567
  46.3 0.0 collective-permute-done.11.recv
  46.3 1.5 %last.1 = (f32[3,64,768]{2,1,0:T(8,128)}, f32[8,3,8,768]{3,2,1,0:T(8,128)S(1)}) custom-call(f32[3,64,768]{2,1,0:T(8,128)S(1)} %get-tuple-element.100.velocity, f32[168,128]{1,0:T(8,128)S(1)} %collective-permute-done.11.recv, s32[6,768]{1,0:T(8,128)S(1)} %get-tuple-element.58.keys, bf16[6,256,768]{2,1,0:T(8,128)(2,1)S(1)} %get-tuple-element.62.hots.rest_0_, ...), custom_call_target="tpu_custom_call" | custom-call | bytes 6000000 | tf_op jit(solution)/shard_map/last/pallas_call | solution.py:567
  47.9 22.4 %all_to_all.5.parts = f32[8,3,8,768]{3,2,1,0:T(8,128)S(1)} all-to-all(f32[8,3,8,768]{3,2,1,0:T(8,128)S(1)} %get-tuple-element.105), channel_id=1, replica_groups=mesh['dom'=4,'event'=8] {'event'}, dimensions={0} | all-to-all | bytes 1179648 | tf_op jit(solution)/shard_map/all_to_all | solution.py:684
  70.2 0.7 event_sum.1
Async XLA Ops:
  0.6 3.9 %copy-start.5 = (bf16[192,192]{1,0:T(8,128)(2,1)S(1)}, bf16[192,192]{1,0:T(8,128)(2,1)}, u32[]{:S(2)}) copy-start(bf16[192,192]{1,0:T(8,128)(2,1)} %constant.24.clone.vel) | copy-start | bytes 221188
  0.6 3.9 %copy-start.2 = (f32[64,768]{1,0:T(8,128)S(1)}, f32[64,768]{1,0:T(8,128)}, u32[]{:S(2)}) copy-start(f32[64,768]{1,0:T(8,128)} %shear.11) | copy-start | bytes 589828
  0.7 3.9 %copy-start.1 = (f32[64,768]{1,0:T(8,128)S(1)}, f32[64,768]{1,0:T(8,128)}, u32[]{:S(2)}) copy-start(f32[64,768]{1,0:T(8,128)} %lame.11) | copy-start | bytes 589828
  3.1 1.4 %collective-permute-start = (f32[168,128]{1,0:T(8,128)S(1)}, f32[168,128]{1,0:T(8,128)S(1)}, u32[]{:S(2)}, u32[]{:S(2)}) collective-permute-start(f32[168,128]{1,0:T(8,128)S(1)} %get-tuple-element.57), channel_id=1, source_target_pairs={{0,8},{8,0},{16,24},{24,16},{1,9},{9,1},{17,25},{25,17},{2,10},{10... | collective-permute-start | bytes 258056 | tf_op jit(solution)/shard_map/ppermute | solution.py:586
  3.6 3.1 %collective-permute-start.1 = (f32[168,128]{1,0:T(8,128)S(1)}, f32[168,128]{1,0:T(8,128)S(1)}, u32[]{:S(2)}, u32[]{:S(2)}) collective-permute-start(f32[168,128]{1,0:T(8,128)S(1)} %get-tuple-element.61), channel_id=1, source_target_pairs={{8,16},{16,8},{9,17},{17,9},{10,18},{18,10},{11,19},{19,11},{12,20... | collective-permute-start | bytes 258056 | tf_op jit(solution)/shard_map/ppermute | solution.py:586
  6.7 6.5 %copy-start = (f32[1,3,3,64,768]{4,3,2,1,0:T(8,128)S(1)}, f32[1,3,3,64,768]{4,3,2,1,0:T(8,128)}, u32[]{:S(2)}) copy-start(f32[1,3,3,64,768]{4,3,2,1,0:T(8,128)} %param.11) | copy-start | bytes 5308420
  6.8 6.5 %copy-start.3 = (f32[64,768]{1,0:T(8,128)S(1)}, f32[64,768]{1,0:T(8,128)}, u32[]{:S(2)}) copy-start(f32[64,768]{1,0:T(8,128)} %density.5) | copy-start | bytes 589828
  6.8 6.5 %copy-start.4 = (bf16[192,192]{1,0:T(8,128)(2,1)S(1)}, bf16[192,192]{1,0:T(8,128)(2,1)}, u32[]{:S(2)}) copy-start(bf16[192,192]{1,0:T(8,128)(2,1)} %constant.25.clone.fwd) | copy-start | bytes 221188
  6.8 6.4 %copy-start.6 = (bf16[64,576]{1,0:T(8,128)(2,1)S(1)}, bf16[64,576]{1,0:T(8,128)(2,1)}, u32[]{:S(2)}) copy-start(bf16[64,576]{1,0:T(8,128)(2,1)} %constant.26.clone.div) | copy-start | bytes 221188
  8.6 4.7 %collective-permute-start.2 = (f32[168,128]{1,0:T(8,128)S(1)}, f32[168,128]{1,0:T(8,128)S(1)}, u32[]{:S(2)}, u32[]{:S(2)}) collective-permute-start(f32[168,128]{1,0:T(8,128)S(1)} %get-tuple-element.71), channel_id=1, source_target_pairs={{0,8},{8,0},{16,24},{24,16},{1,9},{9,1},{17,25},{25,17},{2,10},{10... | collective-permute-start | bytes 258056 | tf_op jit(solution)/shard_map/ppermute | solution.py:586
  12.3 3.3 %collective-permute-start.3 = (f32[168,128]{1,0:T(8,128)S(1)}, f32[168,128]{1,0:T(8,128)S(1)}, u32[]{:S(2)}, u32[]{:S(2)}) collective-permute-start(f32[168,128]{1,0:T(8,128)S(1)} %get-tuple-element.73), channel_id=1, source_target_pairs={{8,16},{16,8},{9,17},{17,9},{10,18},{18,10},{11,19},{19,11},{12,20... | collective-permute-start | bytes 258056 | tf_op jit(solution)/shard_map/ppermute | solution.py:586
  17.3 3.6 %collective-permute-start.4 = (f32[168,128]{1,0:T(8,128)S(1)}, f32[168,128]{1,0:T(8,128)S(1)}, u32[]{:S(2)}, u32[]{:S(2)}) collective-permute-start(f32[168,128]{1,0:T(8,128)S(1)} %get-tuple-element.77), channel_id=1, source_target_pairs={{0,8},{8,0},{16,24},{24,16},{1,9},{9,1},{17,25},{25,17},{2,10},{10... | collective-permute-start | bytes 258056 | tf_op jit(solution)/shard_map/ppermute | solution.py:586
  20.0 3.0 %collective-permute-start.5 = (f32[168,128]{1,0:T(8,128)S(1)}, f32[168,128]{1,0:T(8,128)S(1)}, u32[]{:S(2)}, u32[]{:S(2)}) collective-permute-start(f32[168,128]{1,0:T(8,128)S(1)} %get-tuple-element.80), channel_id=1, source_target_pairs={{8,16},{16,8},{9,17},{17,9},{10,18},{18,10},{11,19},{19,11},{12,20... | collective-permute-start | bytes 258056 | tf_op jit(solution)/shard_map/ppermute | solution.py:586
  24.7 3.8 %collective-permute-start.6 = (f32[168,128]{1,0:T(8,128)S(1)}, f32[168,128]{1,0:T(8,128)S(1)}, u32[]{:S(2)}, u32[]{:S(2)}) collective-permute-start(f32[168,128]{1,0:T(8,128)S(1)} %get-tuple-element.84), channel_id=1, source_target_pairs={{0,8},{8,0},{16,24},{24,16},{1,9},{9,1},{17,25},{25,17},{2,10},{10... | collective-permute-start | bytes 258056 | tf_op jit(solution)/shard_map/ppermute | solution.py:586
  27.6 3.4 %collective-permute-start.7 = (f32[168,128]{1,0:T(8,128)S(1)}, f32[168,128]{1,0:T(8,128)S(1)}, u32[]{:S(2)}, u32[]{:S(2)}) collective-permute-start(f32[168,128]{1,0:T(8,128)S(1)} %get-tuple-element.87), channel_id=1, source_target_pairs={{8,16},{16,8},{9,17},{17,9},{10,18},{18,10},{11,19},{19,11},{12,20... | collective-permute-start | bytes 258056 | tf_op jit(solution)/shard_map/ppermute | solution.py:586
  32.6 3.6 %collective-permute-start.8 = (f32[168,128]{1,0:T(8,128)S(1)}, f32[168,128]{1,0:T(8,128)S(1)}, u32[]{:S(2)}, u32[]{:S(2)}) collective-permute-start(f32[168,128]{1,0:T(8,128)S(1)} %get-tuple-element.90), channel_id=1, source_target_pairs={{0,8},{8,0},{16,24},{24,16},{1,9},{9,1},{17,25},{25,17},{2,10},{10... | collective-permute-start | bytes 258056 | tf_op jit(solution)/shard_map/ppermute | solution.py:586
  35.3 3.0 %collective-permute-start.9 = (f32[168,128]{1,0:T(8,128)S(1)}, f32[168,128]{1,0:T(8,128)S(1)}, u32[]{:S(2)}, u32[]{:S(2)}) collective-permute-start(f32[168,128]{1,0:T(8,128)S(1)} %get-tuple-element.94), channel_id=1, source_target_pairs={{8,16},{16,8},{9,17},{17,9},{10,18},{18,10},{11,19},{19,11},{12,20... | collective-permute-start | bytes 258056 | tf_op jit(solution)/shard_map/ppermute | solution.py:586
  40.1 3.8 %collective-permute-start.10 = (f32[168,128]{1,0:T(8,128)S(1)}, f32[168,128]{1,0:T(8,128)S(1)}, u32[]{:S(2)}, u32[]{:S(2)}) collective-permute-start(f32[168,128]{1,0:T(8,128)S(1)} %get-tuple-element.98), channel_id=1, source_target_pairs={{0,8},{8,0},{16,24},{24,16},{1,9},{9,1},{17,25},{25,17},{2,10},{10... | collective-permute-start | bytes 258056 | tf_op jit(solution)/shard_map/ppermute | solution.py:586
  43.0 3.3 %collective-permute-start.11 = (f32[168,128]{1,0:T(8,128)S(1)}, f32[168,128]{1,0:T(8,128)S(1)}, u32[]{:S(2)}, u32[]{:S(2)}) collective-permute-start(f32[168,128]{1,0:T(8,128)S(1)} %get-tuple-element.101), channel_id=1, source_target_pairs={{8,16},{16,8},{9,17},{17,9},{10,18},{18,10},{11,19},{19,11},{12,20... | collective-permute-start | bytes 258056 | tf_op jit(solution)/shard_map/ppermute | solution.py:586
